TPU v7x, 128 devices: a whole 4x4x4 slice. The times are simulated.
128 devices in a mesh: row: 8 (over y, x_hi), col: 8 (over z, core), slide: 2 (over x_lo).
Axes of the slice: x: 4 (x_hi: 2, x_lo: 2; x = x_hi * 2 + x_lo), y: 4, z: 4, core: 2. Of those that a mesh axis runs over, the one named last changes fastest.
Arguments:
- tokens_in: bfloat16 [2, 128, 128, 256], P('slide', 'row', 'col'), may hold values from -6 to 6
- out_cotangent: bfloat16 [2, 128, 128, 256], P('slide', 'row', 'col'), may hold values from -6 to 6
- w_inner: bfloat16 [256, 1024], replicated, may hold values from -0.375 to 0.375
- w_ssm: bfloat16 [256, 40], replicated, may hold values from -0.375 to 0.375
- dt_bias: float32 [8], replicated, may hold values from -1 to 1
- decay_rate: float32 [8], replicated, may hold values from 0.001 to 0.03
- skip_gain: float32 [8], replicated, may hold values from 0.5 to 1.5
- norm_gain: float32 [512], replicated, may hold values from 0.5 to 1.5
- w_out: bfloat16 [512, 256], replicated, may hold values from -0.25 to 0.25
Outputs:
- layer_out: bfloat16 [2, 128, 128, 256], P('slide', 'row', 'col')
- grad_tokens: bfloat16 [2, 128, 128, 256], P('slide', 'row', 'col')
- grad_inner: float32 [256, 1024], replicated
- grad_ssm: float32 [256, 40], replicated
- grad_out: float32 [512, 256], replicated
- grad_bias: float32 [8], replicated
- grad_rate: float32 [8], replicated
- grad_skip: float32 [8], replicated
- grad_gain: float32 [512], replicated
All inputs are finite; a program needn't handle non-finite values.
Results may differ from a plain program's by a relative error of at most 0.0049.
Values sent between devices are 32-bit elements; how exact they have to be, the bound alone decides.
A program may use at most 128 MiB of HBM per device.

v0:
```python
import jax
import jax.numpy as jnp
from jax import lax
from jax.sharding import PartitionSpec as P

HEADS = 8
HDIM = 64
STATE = 16


highest = lax.Precision.HIGHEST


def from_behind(block, axis, distance):
    devices = range(lax.axis_size(axis))
    route = [(i - distance, i) for i in devices if i - distance in devices]
    return lax.ppermute(block, axis, route)


def split_terms(projected, ssm_proj, dt_bias, decay_rate):
    leading = projected.shape[:-1]
    halfway = projected.shape[-1] // 2
    mixer_in = projected[..., :halfway].reshape(leading + (HEADS, HDIM))
    gate_in = projected[..., halfway:]
    step_size = jax.nn.softplus(ssm_proj[..., 2 * STATE :] + dt_bias)
    return (
        mixer_in,
        gate_in,
        step_size[..., None] * mixer_in,
        -step_size * decay_rate,
        ssm_proj[..., :STATE],
        ssm_proj[..., STATE : 2 * STATE],
    )


def block_out(drive, decay_log, in_map, out_map, state_in):
    cumulative = jnp.cumsum(decay_log, axis=1)
    block_len = drive.shape[1]
    causal = jnp.arange(block_len)[:, None] >= jnp.arange(block_len)[None, :]
    log_gaps = cumulative[:, :, None, :] - cumulative[:, None, :, :]
    decay_mask = jnp.exp(jnp.where(causal[None, :, :, None], log_gaps, -jnp.inf))
    scores = jnp.einsum("sin,sjn->sij", out_map, in_map, precision=highest)
    within = jnp.einsum("sijh,sij,sjhp->sihp", decay_mask, scores, drive, precision=highest)
    carried = jnp.einsum("sin,shpn->sihp", out_map, state_in, precision=highest)
    return within + jnp.exp(cumulative)[..., None] * carried


def block_terms(drive, decay_log, in_map):
    cumulative = jnp.cumsum(decay_log, axis=1)
    final_log = cumulative[:, -1]
    weight = jnp.exp(final_log[:, None, :] - cumulative)
    summary = jnp.einsum("sjh,sjn,sjhp->shpn", weight, in_map, drive, precision=highest)
    return (jnp.exp(final_log), summary)


def rows_view(tensor):
    return tensor.reshape((-1,) + tensor.shape[2:])


def cols_view(tensor):
    swapped = jnp.swapaxes(tensor, 1, 2)
    return swapped.reshape((-1,) + swapped.shape[2:])


def cols_back(tensor, slides):
    return jnp.swapaxes(tensor.reshape((slides, -1) + tensor.shape[1:]), 1, 2)


def edge_terms(projected, ssm_proj, dt_bias, decay_rate):
    mixer_in, gate_in, drive, decay_log, in_map, out_map = split_terms(
        projected, ssm_proj, dt_bias, decay_rate
    )
    decay_row, fresh_row = block_terms(rows_view(drive), rows_view(decay_log), rows_view(in_map))
    decay_col, fresh_col = block_terms(cols_view(drive), cols_view(decay_log), cols_view(in_map))
    return (decay_row, fresh_row, decay_col, fresh_col)


def local_layer(projected, ssm_proj, dt_bias, decay_rate, skip_gain, norm_gain, in_row, in_col):
    mixer_in, gate_in, drive, decay_log, in_map, out_map = split_terms(
        projected, ssm_proj, dt_bias, decay_rate
    )
    terms = (drive, decay_log, in_map, out_map)
    row_terms = [rows_view(tensor) for tensor in terms]
    col_terms = [cols_view(tensor) for tensor in terms]
    row_out = block_out(*row_terms, in_row).reshape(drive.shape)
    col_out = cols_back(block_out(*col_terms, in_col), projected.shape[0])
    mixed = row_out + col_out + skip_gain[:, None] * mixer_in
    gated = mixed.reshape(projected.shape[:-1] + (-1,)) * jax.nn.silu(gate_in)
    inv_rms = lax.rsqrt(jnp.mean(gated * gated, axis=-1, keepdims=True) + 1e-05)
    return gated * inv_rms * norm_gain


def outer_sum(left, right):
    return lax.dot_general(
        left, right, (((0,), (0,)), ((), ())), preferred_element_type=jnp.float32
    )


def local(
    tokens_in, out_cotangent, w_inner, w_ssm, dt_bias, decay_rate, skip_gain, norm_gain, w_out
):
    slides, tile_rows, tile_cols, width = tokens_in.shape
    tokens = tokens_in.reshape(-1, width)
    cotangent = out_cotangent.reshape(-1, width)
    projected = jnp.dot(tokens, w_inner, preferred_element_type=jnp.float32).reshape(
        slides, tile_rows, tile_cols, -1
    )
    ssm_proj = jnp.dot(tokens, w_ssm, preferred_element_type=jnp.float32).reshape(
        slides, tile_rows, tile_cols, -1
    )
    edges, edge_pull = jax.vjp(edge_terms, projected, ssm_proj, dt_bias, decay_rate)
    decay_row, fresh_row, decay_col, fresh_col = edges
    in_row = jnp.zeros_like(fresh_row)
    in_col = jnp.zeros_like(fresh_col)
    for advance in range(lax.axis_size("col") - 1):
        in_row = from_behind(decay_row[..., None, None] * in_row + fresh_row, "col", 1)
    for advance in range(lax.axis_size("row") - 1):
        in_col = from_behind(decay_col[..., None, None] * in_col + fresh_col, "row", 1)
    normed_f, pullback = jax.vjp(
        local_layer, projected, ssm_proj, dt_bias, decay_rate, skip_gain, norm_gain, in_row, in_col
    )
    normed = normed_f.astype(jnp.bfloat16).reshape(-1, w_out.shape[0])
    layer_out = (
        jnp.dot(normed, w_out, preferred_element_type=jnp.float32)
        .astype(jnp.bfloat16)
        .reshape(tokens_in.shape)
    )
    d_normed = lax.dot_general(
        cotangent, w_out, (((1,), (1,)), ((), ())), preferred_element_type=jnp.float32
    )
    first = pullback(d_normed.reshape(normed_f.shape))
    own_row = first[6]
    own_col = first[7]
    back_row = jnp.zeros_like(own_row)
    back_col = jnp.zeros_like(own_col)
    for advance in range(lax.axis_size("col") - 1):
        back_row = from_behind(decay_row[..., None, None] * back_row + own_row, "col", -1)
    for advance in range(lax.axis_size("row") - 1):
        back_col = from_behind(decay_col[..., None, None] * back_col + own_col, "row", -1)
    second = edge_pull(
        (
            jnp.sum(back_row * in_row, axis=(-2, -1)),
            back_row,
            jnp.sum(back_col * in_col, axis=(-2, -1)),
            back_col,
        )
    )
    grads = [first[which] + second[which] for which in range(4)] + [first[4], first[5]]
    d_proj = grads[0].reshape(-1, w_inner.shape[1]).astype(jnp.bfloat16)
    d_ssm = grads[1].reshape(-1, w_ssm.shape[1]).astype(jnp.bfloat16)
    back_proj = lax.dot_general(
        d_proj, w_inner, (((1,), (1,)), ((), ())), preferred_element_type=jnp.float32
    )
    back_proj = back_proj + lax.dot_general(
        d_ssm, w_ssm, (((1,), (1,)), ((), ())), preferred_element_type=jnp.float32
    )
    grad_tokens = back_proj.astype(jnp.bfloat16).reshape(tokens_in.shape)
    summed = lax.psum(
        (
            outer_sum(tokens, d_proj),
            outer_sum(tokens, d_ssm),
            outer_sum(normed, cotangent),
            grads[2],
            grads[3],
            grads[4],
            grads[5],
        ),
        ("row", "col", "slide"),
    )
    token_total = (
        lax.axis_size("slide")
        * lax.axis_size("row")
        * lax.axis_size("col")
        * slides
        * tile_rows
        * tile_cols
    )
    factor = 1.0 / jnp.sqrt(jnp.float32(token_total))
    return (
        layer_out,
        grad_tokens,
        summed[0] * factor,
        summed[1] * factor,
        summed[2] * factor,
        summed[3] * factor,
        summed[4] * factor,
        summed[5] * factor,
        summed[6] * factor,
    )


def solution(mesh):
    in_specs = (
        P("slide", "row", "col", None),
        P("slide", "row", "col", None),
        P(),
        P(),
        P(),
        P(),
        P(),
        P(),
        P(),
    )
    out_specs = (
        P("slide", "row", "col", None),
        P("slide", "row", "col", None),
        P(),
        P(),
        P(),
        P(),
        P(),
        P(),
        P(),
    )
    return jax.shard_map(local, mesh=mesh, in_specs=in_specs, out_specs=out_specs, check_vma=False)
```

profile of v0, /device:TPU:1, one launch (start us, length us, event | category | flops | bytes accessed | tf_op | source)
XLA Modules:
  0.0 732.7 jit_solution(16848153442287800627)
XLA Ops:
  13.2 4.4 broadcast_add_fusion.3
  17.7 4.9 collective-permute-start
  26.6 3.5 broadcast_add_fusion.1
  30.2 5.6 collective-permute-start.7
  38.0 2.5 collective-permute-start.1
  40.5 17.4 %collective-permute-done.7 = f32[16,8,64,16]{2,3,1,0:T(8,128)} collective-permute-done((f32[16,8,64,16]{2,3,1,0:T(8,128)}, f32[16,8,64,16]{2,3,1,0:T(8,128)}, u32[]{:S(2)}, u32[]{:S(2)}) %collective-permute-start.7) | collective-permute-done | bytes 524320 | tf_op jit(solution)/shard_map/ppermute | solution.py:17
  59.3 5.5 collective-permute-start.8
  66.0 2.6 collective-permute-start.2
  68.5 18.3 %collective-permute-done.8 = f32[16,8,64,16]{2,3,1,0:T(8,128)S(1)} collective-permute-done((f32[16,8,64,16]{2,3,1,0:T(8,128)S(1)}, f32[16,8,64,16]{2,3,1,0:T(8,128)S(1)}, u32[]{:S(2)}, u32[]{:S(2)}) %collective-permute-start.8) | collective-permute-done | bytes 524320 | tf_op jit(solution)/shard_map/ppermute | solution.py:17
  88.0 6.7 collective-permute-start.9
  101.3 4.2 collective-permute-start.3
  105.5 9.8 %collective-permute-done.9 = f32[16,8,64,16]{2,3,1,0:T(8,128)} collective-permute-done((f32[16,8,64,16]{2,3,1,0:T(8,128)}, f32[16,8,64,16]{2,3,1,0:T(8,128)}, u32[]{:S(2)}, u32[]{:S(2)}) %collective-permute-start.9) | collective-permute-done | bytes 524320 | tf_op jit(solution)/shard_map/ppermute | solution.py:17
  116.7 5.7 collective-permute-start.10
  123.1 5.8 collective-permute-start.4
  129.0 13.7 %collective-permute-done.10 = f32[16,8,64,16]{2,3,1,0:T(8,128)S(1)} collective-permute-done((f32[16,8,64,16]{2,3,1,0:T(8,128)S(1)}, f32[16,8,64,16]{2,3,1,0:T(8,128)S(1)}, u32[]{:S(2)}, u32[]{:S(2)}) %collective-permute-start.10) | collective-permute-done | bytes 524320 | tf_op jit(solution)/shard_map/ppermute | solution.py:17
  142.9 6.2 collective-permute-start.11
  149.1 1.8 fusion.29
  151.2 7.4 %collective-permute-start.5 = (f32[16,8,64,16]{2,3,1,0:T(8,128)S(1)}, f32[16,8,64,16]{2,3,1,0:T(8,128)S(1)}, u32[]{:S(2)}, u32[]{:S(2)}) collective-permute-start(f32[16,8,64,16]{2,3,1,0:T(8,128)S(1)} %multiply_add_fusion.20), channel_id=1, source_target_pairs={{0,2},{2,4},{4,6},{6,8},{8,10},{10,12},{12,14},{1,3},{3,5},{5,7},{... | collective-permute-start | bytes 1572872 | tf_op jit(solution)/shard_map/ppermute | solution.py:17
  158.6 9.5 %collective-permute-done.11 = f32[16,8,64,16]{2,3,1,0:T(8,128)S(1)} collective-permute-done((f32[16,8,64,16]{2,3,1,0:T(8,128)S(1)}, f32[16,8,64,16]{2,3,1,0:T(8,128)S(1)}, u32[]{:S(2)}, u32[]{:S(2)}) %collective-permute-start.11) | collective-permute-done | bytes 524320 | tf_op jit(solution)/shard_map/ppermute | solution.py:17
  168.3 6.6 collective-permute-start.12
  175.5 9.3 %collective-permute-start.6 = (f32[16,8,64,16]{2,3,1,0:T(8,128)S(1)}, f32[16,8,64,16]{2,3,1,0:T(8,128)S(1)}, u32[]{:S(2)}, u32[]{:S(2)}) collective-permute-start(f32[16,8,64,16]{2,3,1,0:T(8,128)S(1)} %multiply_add_fusion.19), channel_id=1, source_target_pairs={{0,2},{2,4},{4,6},{6,8},{8,10},{10,12},{12,14},{1,3},{3,5},{5,7},{... | collective-permute-start | bytes 1572872 | tf_op jit(solution)/shard_map/ppermute | solution.py:17
  184.9 8.4 %collective-permute-done.12 = f32[16,8,64,16]{2,3,1,0:T(8,128)S(1)} collective-permute-done((f32[16,8,64,16]{2,3,1,0:T(8,128)S(1)}, f32[16,8,64,16]{2,3,1,0:T(8,128)S(1)}, u32[]{:S(2)}, u32[]{:S(2)}) %collective-permute-start.12) | collective-permute-done | bytes 524320 | tf_op jit(solution)/shard_map/ppermute | solution.py:17
  193.5 6.6 collective-permute-start.13
  202.5 15.0 %collective-permute-done.13 = f32[16,8,64,16]{2,3,1,0:T(8,128)S(1)} collective-permute-done((f32[16,8,64,16]{2,3,1,0:T(8,128)S(1)}, f32[16,8,64,16]{2,3,1,0:T(8,128)S(1)}, u32[]{:S(2)}, u32[]{:S(2)}) %collective-permute-start.13) | collective-permute-done | bytes 524320 | tf_op jit(solution)/shard_map/ppermute | solution.py:17
  219.6 3.3 fusion.18
  224.3 2.4 reshape.443
  229.7 2.1 multiply_reduce_fusion.8
  236.0 3.1 convolution_bitcast_fusion.1
  239.1 2.4 broadcast_add_fusion.2
  242.3 11.3 %fusion.23 = (f32[16,16,8]{0,2,1:T(8,128)S(1)}, f32[16,16,8,64]{3,0,2,1:T(8,128)}) fusion(f32[16,16,8,64]{3,1,2,0:T(8,128)} %copy-done.15, f32[1,16,16,8,64]{4,3,2,1,0:T(8,128)} %reshape.448, f32[16,16,8]{0,2,1:T(8,128)S(1)} %copy-done.67), kind=kLoop, calls=%fused_computation.45 | loop fusion | flops 391168 | bytes 1589248 | tf_op jit(solution)/shard_map/transpose(jvp())/reduce_sum | solution.py:45
  254.5 4.0 broadcast_add_fusion
  258.6 3.5 fusion.27
  262.0 4.0 fusion.54
  266.7 1.6 copy.308
  270.7 7.7 %collective-permute-start.21 = (f32[16,8,64,16]{2,3,1,0:T(8,128)}, f32[16,8,64,16]{2,3,1,0:T(8,128)S(1)}, u32[]{:S(2)}, u32[]{:S(2)}) collective-permute-start(f32[16,8,64,16]{2,3,1,0:T(8,128)} %get-tuple-element.109), channel_id=1, source_target_pairs={{2,0},{4,2},{6,4},{8,6},{10,8},{12,10},{14,12},{3,1},{5,3},{7,5},{... | collective-permute-start | bytes 1572872 | tf_op jit(solution)/shard_map/ppermute | solution.py:17
  279.9 3.6 convolution_bitcast_fusion.10
  284.2 3.7 fusion.11
  287.9 8.2 %collective-permute-done.21 = f32[16,8,64,16]{2,3,1,0:T(8,128)S(1)} collective-permute-done((f32[16,8,64,16]{2,3,1,0:T(8,128)}, f32[16,8,64,16]{2,3,1,0:T(8,128)S(1)}, u32[]{:S(2)}, u32[]{:S(2)}) %collective-permute-start.21) | collective-permute-done | bytes 524320 | tf_op jit(solution)/shard_map/ppermute | solution.py:17
  296.3 2.3 collective-permute-start.22
  298.6 2.3 bitcast_add_fusion.4
  300.9 7.5 %collective-permute-done.14 = f32[16,8,64,16]{2,3,1,0:T(8,128)S(1)} collective-permute-done((f32[16,8,64,16]{2,3,1,0:T(8,128)}, f32[16,8,64,16]{2,3,1,0:T(8,128)S(1)}, u32[]{:S(2)}, u32[]{:S(2)}) %collective-permute-start.14) | collective-permute-done | bytes 524320 | tf_op jit(solution)/shard_map/ppermute | solution.py:17
  310.0 2.5 collective-permute-done.22
  312.8 1.9 collective-permute-start.23
  315.6 22.9 %collective-permute-done.15 = f32[16,8,64,16]{2,3,1,0:T(8,128)S(1)} collective-permute-done((f32[16,8,64,16]{2,3,1,0:T(8,128)S(1)}, f32[16,8,64,16]{2,3,1,0:T(8,128)S(1)}, u32[]{:S(2)}, u32[]{:S(2)}) %collective-permute-start.15) | collective-permute-done | bytes 524320 | tf_op jit(solution)/shard_map/ppermute | solution.py:17
  340.4 2.7 collective-permute-start.24
  343.6 23.1 %collective-permute-done.16 = f32[16,8,64,16]{2,3,1,0:T(8,128)S(1)} collective-permute-done((f32[16,8,64,16]{2,3,1,0:T(8,128)S(1)}, f32[16,8,64,16]{2,3,1,0:T(8,128)S(1)}, u32[]{:S(2)}, u32[]{:S(2)}) %collective-permute-start.16) | collective-permute-done | bytes 524320 | tf_op jit(solution)/shard_map/ppermute | solution.py:17
  368.4 3.7 collective-permute-start.25
  373.2 20.5 %collective-permute-done.17 = f32[16,8,64,16]{2,3,1,0:T(8,128)S(1)} collective-permute-done((f32[16,8,64,16]{2,3,1,0:T(8,128)S(1)}, f32[16,8,64,16]{2,3,1,0:T(8,128)S(1)}, u32[]{:S(2)}, u32[]{:S(2)}) %collective-permute-start.17) | collective-permute-done | bytes 524320 | tf_op jit(solution)/shard_map/ppermute | solution.py:17
  395.7 4.6 collective-permute-start.26
  400.4 19.7 %collective-permute-done.18 = f32[16,8,64,16]{2,3,1,0:T(8,128)S(1)} collective-permute-done((f32[16,8,64,16]{2,3,1,0:T(8,128)S(1)}, f32[16,8,64,16]{2,3,1,0:T(8,128)S(1)}, u32[]{:S(2)}, u32[]{:S(2)}) %collective-permute-start.18) | collective-permute-done | bytes 524320 | tf_op jit(solution)/shard_map/ppermute | solution.py:17
  424.0 5.7 collective-permute-start.27
  431.8 15.1 %collective-permute-done.19 = f32[16,8,64,16]{2,3,1,0:T(8,128)} collective-permute-done((f32[16,8,64,16]{2,3,1,0:T(8,128)}, f32[16,8,64,16]{2,3,1,0:T(8,128)}, u32[]{:S(2)}, u32[]{:S(2)}) %collective-permute-start.19) | collective-permute-done | bytes 524320 | tf_op jit(solution)/shard_map/ppermute | solution.py:17
  446.9 2.5 multiply_add_fusion.6
  449.4 1.7 collective-permute-start.20
  451.1 1.6 multiply_reduce_fusion.3
  452.7 4.2 fusion.20
  460.8 13.0 %collective-permute-done.20 = f32[16,8,64,16]{2,3,1,0:T(8,128)S(1)} collective-permute-done((f32[16,8,64,16]{2,3,1,0:T(8,128)}, f32[16,8,64,16]{2,3,1,0:T(8,128)S(1)}, u32[]{:S(2)}, u32[]{:S(2)}) %collective-permute-start.20) | collective-permute-done | bytes 524320 | tf_op jit(solution)/shard_map/ppermute | solution.py:17
  473.8 1.9 multiply_reduce_fusion.4
  475.8 3.3 fusion.22
  483.2 2.6 fusion
  485.8 4.7 multiply_reduce_fusion.5
  492.5 1.9 multiply_reduce_fusion.11
  496.3 73.7 %all-reduce.10 = (f32[256,40]{0,1:T(8,128)S(1)}, f32[8]{0:T(128)S(1)}, f32[8]{0:T(128)S(1)}, f32[8]{0:T(128)S(1)}, f32[512]{0:T(512)S(1)}) all-reduce(f32[256,40]{0,1:T(8,128)S(1)} %convolution_bitcast_fusion.11, f32[8]{0:T(128)S(1)} %add.218, f32[8]{0:T(128)S(1)} %add.219, ...), channel_id=1, replica_groups=mesh['row'=8,'col'=8,'slide'=2] {'row','col','slide'}, use_global_device_ids=true, to_apply=%region_21.23 | all-reduce | flops 10776 | bytes 86208 | tf_op jit(solution)/shard_map/psum | solution.py:158
  578.1 143.8 %all-reduce.14.cloned.1.call-done = (f32[256,1024]{0,1:T(8,128)}, f32[512,256]{1,0:T(8,128)}) async-done(((f32[256,1024]{0,1:T(8,128)}, f32[512,256]{1,0:T(8,128)}), (f32[256,1024]{0,1:T(8,128)}, f32[512,256]{1,0:T(8,128)})) %all-reduce.14.cloned.1.call-update) | async-done | bytes 1572880 | tf_op jit(solution)/shard_map/psum | solution.py:158
  (374 shorter events, 85.2 us)
Async XLA Ops:
  7.2 714.7 %all-reduce.14.cloned.1.call-start = ((), (), s32[]{:S(2)}) async-start(), calls=%async_computation | async-start | bytes 3145728 | tf_op jit(solution)/shard_map/psum | solution.py:158
  17.7 18.9 %collective-permute-start = (f32[16,8,64,16]{2,3,1,0:T(8,128)}, f32[16,8,64,16]{2,3,1,0:T(8,128)}, u32[]{:S(2)}, u32[]{:S(2)}) collective-permute-start(f32[16,8,64,16]{2,3,1,0:T(8,128)} %get-tuple-element.99), channel_id=1, source_target_pairs={{0,2},{2,4},{4,6},{6,8},{8,10},{10,12},{12,14},{1,3},{3,5},{5,7},{... | collective-permute-start | bytes 1572872 | tf_op jit(solution)/shard_map/ppermute | solution.py:17
  26.6 9.2 %copy-start.104 = (f32[16,8]{0,1:T(8,128)S(1)}, f32[16,8]{0,1:T(8,128)}, u32[]{:S(2)}) copy-start(f32[16,8]{0,1:T(8,128)} %get-tuple-element.97) | copy-start | bytes 1540
  30.2 27.7 %collective-permute-start.7 = (f32[16,8,64,16]{2,3,1,0:T(8,128)}, f32[16,8,64,16]{2,3,1,0:T(8,128)}, u32[]{:S(2)}, u32[]{:S(2)}) collective-permute-start(f32[16,8,64,16]{2,3,1,0:T(8,128)} %get-tuple-element.101), channel_id=1, source_target_pairs={{0,16},{16,32},{32,48},{48,64},{64,80},{80,96},{96,112},{1,17},{17... | collective-permute-start | bytes 1572872 | tf_op jit(solution)/shard_map/ppermute | solution.py:17
  38.0 26.8 %collective-permute-start.1 = (f32[16,8,64,16]{2,3,1,0:T(8,128)S(1)}, f32[16,8,64,16]{2,3,1,0:T(8,128)S(1)}, u32[]{:S(2)}, u32[]{:S(2)}) collective-permute-start(f32[16,8,64,16]{2,3,1,0:T(8,128)S(1)} %multiply_add_fusion.24), channel_id=1, source_target_pairs={{0,2},{2,4},{4,6},{6,8},{8,10},{10,12},{12,14},{1,3},{3,5},{5,7},{... | collective-permute-start | bytes 1572872 | tf_op jit(solution)/shard_map/ppermute | solution.py:17
  59.3 27.5 %collective-permute-start.8 = (f32[16,8,64,16]{2,3,1,0:T(8,128)S(1)}, f32[16,8,64,16]{2,3,1,0:T(8,128)S(1)}, u32[]{:S(2)}, u32[]{:S(2)}) collective-permute-start(f32[16,8,64,16]{2,3,1,0:T(8,128)S(1)} %multiply_add_fusion.18), channel_id=1, source_target_pairs={{0,16},{16,32},{32,48},{48,64},{64,80},{80,96},{96,112},{1,17},{17... | collective-permute-start | bytes 1572872 | tf_op jit(solution)/shard_map/ppermute | solution.py:17
  66.0 28.8 %copy-start.32 = (f32[16,16,8]{2,0,1:T(8,128)S(1)}, f32[16,16,8]{2,0,1:T(8,128)}, u32[]{:S(2)}) copy-start(f32[16,16,8]{2,0,1:T(8,128)} %copy-done.31) | copy-start | bytes 24580
  66.0 33.9 %collective-permute-start.2 = (f32[16,8,64,16]{2,3,1,0:T(8,128)}, f32[16,8,64,16]{2,3,1,0:T(8,128)}, u32[]{:S(2)}, u32[]{:S(2)}) collective-permute-start(f32[16,8,64,16]{2,3,1,0:T(8,128)} %multiply_add_fusion.23), channel_id=1, source_target_pairs={{0,2},{2,4},{4,6},{6,8},{8,10},{10,12},{12,14},{1,3},{3,5},{5,7},{... | collective-permute-start | bytes 1572872 | tf_op jit(solution)/shard_map/ppermute | solution.py:17
  88.0 6.8 copy-start.36
  88.0 27.3 %collective-permute-start.9 = (f32[16,8,64,16]{2,3,1,0:T(8,128)}, f32[16,8,64,16]{2,3,1,0:T(8,128)}, u32[]{:S(2)}, u32[]{:S(2)}) collective-permute-start(f32[16,8,64,16]{2,3,1,0:T(8,128)} %multiply_add_fusion.17), channel_id=1, source_target_pairs={{0,16},{16,32},{32,48},{48,64},{64,80},{80,96},{96,112},{1,17},{17... | collective-permute-start | bytes 1572872 | tf_op jit(solution)/shard_map/ppermute | solution.py:17
  95.8 53.2 %copy-start.38 = (f32[16,16,8]{1,2,0:T(8,128)}, f32[16,16,8]{1,2,0:T(8,128)S(1)}, u32[]{:S(2)}) copy-start(f32[16,16,8]{1,2,0:T(8,128)S(1)} %copy.261) | copy-start | bytes 24580
  99.9 119.6 %copy-start.101 = (pred[16,16]{1,0:T(8,128)(4,1)}, pred[16,16]{1,0:T(8,128)(4,1)S(1)}, u32[]{:S(2)}) copy-start(pred[16,16]{1,0:T(8,128)(4,1)S(1)} %iota_compare_fusion) | copy-start | bytes 772
  101.3 21.1 %copy-start.46 = (f32[16,16,16]{2,0,1:T(8,128)S(1)}, f32[16,16,16]{2,0,1:T(8,128)}, u32[]{:S(2)}) copy-start(f32[16,16,16]{2,0,1:T(8,128)} %get-tuple-element.92) | copy-start | bytes 49156
  101.3 21.5 %collective-permute-start.3 = (f32[16,8,64,16]{2,3,1,0:T(8,128)S(1)}, f32[16,8,64,16]{2,3,1,0:T(8,128)S(1)}, u32[]{:S(2)}, u32[]{:S(2)}) collective-permute-start(f32[16,8,64,16]{2,3,1,0:T(8,128)S(1)} %multiply_add_fusion.22), channel_id=1, source_target_pairs={{0,2},{2,4},{4,6},{6,8},{8,10},{10,12},{12,14},{1,3},{3,5},{5,7},{... | collective-permute-start | bytes 1572872 | tf_op jit(solution)/shard_map/ppermute | solution.py:17
  116.7 25.9 %collective-permute-start.10 = (f32[16,8,64,16]{2,3,1,0:T(8,128)S(1)}, f32[16,8,64,16]{2,3,1,0:T(8,128)S(1)}, u32[]{:S(2)}, u32[]{:S(2)}) collective-permute-start(f32[16,8,64,16]{2,3,1,0:T(8,128)S(1)} %multiply_add_fusion.16), channel_id=1, source_target_pairs={{0,16},{16,32},{32,48},{48,64},{64,80},{80,96},{96,112},{1,17},{17... | collective-permute-start | bytes 1572872 | tf_op jit(solution)/shard_map/ppermute | solution.py:17
  122.8 26.2 %copy-start.50 = (f32[16,16,16]{2,1,0:T(8,128)}, f32[16,16,16]{2,1,0:T(8,128)S(1)}, u32[]{:S(2)}) copy-start(f32[16,16,16]{2,1,0:T(8,128)S(1)} %fusion.132) | copy-start | bytes 49156
  123.1 26.0 %copy-start.7 = (f32[16,16,8,64]{3,0,2,1:T(8,128)S(1)}, f32[16,16,8,64]{3,0,2,1:T(8,128)}, u32[]{:S(2)}) copy-start(f32[16,16,8,64]{3,0,2,1:T(8,128)} %copy-done.6) | copy-start | bytes 1572868
  123.1 27.8 %collective-permute-start.4 = (f32[16,8,64,16]{2,3,1,0:T(8,128)S(1)}, f32[16,8,64,16]{2,3,1,0:T(8,128)S(1)}, u32[]{:S(2)}, u32[]{:S(2)}) collective-permute-start(f32[16,8,64,16]{2,3,1,0:T(8,128)S(1)} %multiply_add_fusion.21), channel_id=1, source_target_pairs={{0,2},{2,4},{4,6},{6,8},{8,10},{10,12},{12,14},{1,3},{3,5},{5,7},{... | collective-permute-start | bytes 1572872 | tf_op jit(solution)/shard_map/ppermute | solution.py:17
  142.9 25.2 %collective-permute-start.11 = (f32[16,8,64,16]{2,3,1,0:T(8,128)S(1)}, f32[16,8,64,16]{2,3,1,0:T(8,128)S(1)}, u32[]{:S(2)}, u32[]{:S(2)}) collective-permute-start(f32[16,8,64,16]{2,3,1,0:T(8,128)S(1)} %multiply_add_fusion.15), channel_id=1, source_target_pairs={{0,16},{16,32},{32,48},{48,64},{64,80},{80,96},{96,112},{1,17},{17... | collective-permute-start | bytes 1572872 | tf_op jit(solution)/shard_map/ppermute | solution.py:17
  151.2 24.1 %collective-permute-start.5 = (f32[16,8,64,16]{2,3,1,0:T(8,128)S(1)}, f32[16,8,64,16]{2,3,1,0:T(8,128)S(1)}, u32[]{:S(2)}, u32[]{:S(2)}) collective-permute-start(f32[16,8,64,16]{2,3,1,0:T(8,128)S(1)} %multiply_add_fusion.20), channel_id=1, source_target_pairs={{0,2},{2,4},{4,6},{6,8},{8,10},{10,12},{12,14},{1,3},{3,5},{5,7},{... | collective-permute-start | bytes 1572872 | tf_op jit(solution)/shard_map/ppermute | solution.py:17
  168.3 25.0 %collective-permute-start.12 = (f32[16,8,64,16]{2,3,1,0:T(8,128)S(1)}, f32[16,8,64,16]{2,3,1,0:T(8,128)S(1)}, u32[]{:S(2)}, u32[]{:S(2)}) collective-permute-start(f32[16,8,64,16]{2,3,1,0:T(8,128)S(1)} %multiply_add_fusion.14), channel_id=1, source_target_pairs={{0,16},{16,32},{32,48},{48,64},{64,80},{80,96},{96,112},{1,17},{17... | collective-permute-start | bytes 1572872 | tf_op jit(solution)/shard_map/ppermute | solution.py:17
  175.3 44.3 %copy-start.40 = (f32[16,16,16]{2,1,0:T(8,128)}, f32[16,16,16]{2,1,0:T(8,128)S(1)}, u32[]{:S(2)}) copy-start(f32[16,16,16]{2,1,0:T(8,128)S(1)} %fusion.114) | copy-start | bytes 49156
  175.5 24.5 %copy-start.63 = (bf16[512,256]{1,0:T(8,128)(2,1)S(1)}, bf16[512,256]{1,0:T(8,128)(2,1)}, u32[]{:S(2)}) copy-start(bf16[512,256]{1,0:T(8,128)(2,1)} %param.18) | copy-start | bytes 786436
  175.5 24.5 %copy-start.87 = (bf16[1,16,16,256]{3,2,1,0:T(8,128)(2,1)S(1)}, bf16[1,16,16,256]{3,2,1,0:T(8,128)(2,1)}, u32[]{:S(2)}) copy-start(bf16[1,16,16,256]{3,2,1,0:T(8,128)(2,1)} %param.11) | copy-start | bytes 393220
  175.5 24.8 %collective-permute-start.6 = (f32[16,8,64,16]{2,3,1,0:T(8,128)S(1)}, f32[16,8,64,16]{2,3,1,0:T(8,128)S(1)}, u32[]{:S(2)}, u32[]{:S(2)}) collective-permute-start(f32[16,8,64,16]{2,3,1,0:T(8,128)S(1)} %multiply_add_fusion.19), channel_id=1, source_target_pairs={{0,2},{2,4},{4,6},{6,8},{8,10},{10,12},{12,14},{1,3},{3,5},{5,7},{... | collective-permute-start | bytes 1572872 | tf_op jit(solution)/shard_map/ppermute | solution.py:17
  193.5 24.0 %collective-permute-start.13 = (f32[16,8,64,16]{2,3,1,0:T(8,128)S(1)}, f32[16,8,64,16]{2,3,1,0:T(8,128)S(1)}, u32[]{:S(2)}, u32[]{:S(2)}) collective-permute-start(f32[16,8,64,16]{2,3,1,0:T(8,128)S(1)} %multiply_add_fusion.13), channel_id=1, source_target_pairs={{0,16},{16,32},{32,48},{48,64},{64,80},{80,96},{96,112},{1,17},{17... | collective-permute-start | bytes 1572872 | tf_op jit(solution)/shard_map/ppermute | solution.py:17
  200.4 18.1 %copy-start.44 = (f32[16,16,16,1]{1,2,3,0:T(8,128)S(1)}, f32[16,16,16,1]{1,2,3,0:T(8,128)}, u32[]{:S(2)}) copy-start(f32[16,16,16,1]{1,2,3,0:T(8,128)} %copy.336) | copy-start | bytes 49156
  201.4 18.2 %copy-start.113 = (f32[8]{0:T(128)S(1)}, f32[8]{0:T(128)}, u32[]{:S(2)}) copy-start(f32[8]{0:T(128)} %param.16) | copy-start | bytes 100
  202.4 17.1 %copy-start.19 = (f32[16,16,8,64]{3,1,2,0:T(8,128)}, f32[16,16,8,64]{3,1,2,0:T(8,128)S(1)}, u32[]{:S(2)}) copy-start(f32[16,16,8,64]{3,1,2,0:T(8,128)S(1)} %fusion.105) | copy-start | bytes 1572868
  202.5 17.1 %copy-start.4 = (f32[16,16,8,64]{3,2,1,0:T(8,128)S(1)}, f32[16,16,8,64]{3,2,1,0:T(8,128)}, u32[]{:S(2)}) copy-start(f32[16,16,8,64]{3,2,1,0:T(8,128)} %copy-done.3) | copy-start | bytes 1572868
  202.5 17.1 %copy-start.11 = (f32[1,16,16,8,64]{4,3,2,1,0:T(8,128)S(1)}, f32[1,16,16,8,64]{4,3,2,1,0:T(8,128)}, u32[]{:S(2)}) copy-start(f32[1,16,16,8,64]{4,3,2,1,0:T(8,128)} %copy-done.10) | copy-start | bytes 1572868
  202.5 17.1 %copy-start.57 = (f32[16,16,8]{1,2,0:T(8,128)S(1)}, f32[16,16,8]{1,2,0:T(8,128)}, u32[]{:S(2)}) copy-start(f32[16,16,8]{1,2,0:T(8,128)} %copy.254) | copy-start | bytes 24580
  202.5 17.1 %copy-start.66 = (f32[16,16,8]{0,2,1:T(8,128)S(1)}, f32[16,16,8]{0,2,1:T(8,128)}, u32[]{:S(2)}) copy-start(f32[16,16,8]{0,2,1:T(8,128)} %copy.269) | copy-start | bytes 24580
  233.1 6.0 copy-start.1
  270.7 25.3 %collective-permute-start.21 = (f32[16,8,64,16]{2,3,1,0:T(8,128)}, f32[16,8,64,16]{2,3,1,0:T(8,128)S(1)}, u32[]{:S(2)}, u32[]{:S(2)}) collective-permute-start(f32[16,8,64,16]{2,3,1,0:T(8,128)} %get-tuple-element.109), channel_id=1, source_target_pairs={{2,0},{4,2},{6,4},{8,6},{10,8},{12,10},{14,12},{3,1},{5,3},{7,5},{... | collective-permute-start | bytes 1572872 | tf_op jit(solution)/shard_map/ppermute | solution.py:17
  278.5 5.3 copy-start.2
  278.5 29.8 %collective-permute-start.14 = (f32[16,8,64,16]{2,3,1,0:T(8,128)}, f32[16,8,64,16]{2,3,1,0:T(8,128)S(1)}, u32[]{:S(2)}, u32[]{:S(2)}) collective-permute-start(f32[16,8,64,16]{2,3,1,0:T(8,128)} %get-tuple-element.107), channel_id=1, source_target_pairs={{16,0},{32,16},{48,32},{64,48},{80,64},{96,80},{112,96},{17,1},{33... | collective-permute-start | bytes 1572872 | tf_op jit(solution)/shard_map/ppermute | solution.py:17
  296.3 16.2 %collective-permute-start.22 = (f32[16,8,64,16]{2,3,1,0:T(8,128)S(1)}, f32[16,8,64,16]{2,3,1,0:T(8,128)S(1)}, u32[]{:S(2)}, u32[]{:S(2)}) collective-permute-start(f32[16,8,64,16]{2,3,1,0:T(8,128)S(1)} %multiply_add_fusion.5), channel_id=1, source_target_pairs={{2,0},{4,2},{6,4},{8,6},{10,8},{12,10},{14,12},{3,1},{5,3},{7,5},{... | collective-permute-start | bytes 1572872 | tf_op jit(solution)/shard_map/ppermute | solution.py:17
  308.6 6.2 copy-start.64
  308.6 6.2 copy-start.65
  308.6 29.9 %collective-permute-start.15 = (f32[16,8,64,16]{2,3,1,0:T(8,128)S(1)}, f32[16,8,64,16]{2,3,1,0:T(8,128)S(1)}, u32[]{:S(2)}, u32[]{:S(2)}) collective-permute-start(f32[16,8,64,16]{2,3,1,0:T(8,128)S(1)} %multiply_add_fusion.11), channel_id=1, source_target_pairs={{16,0},{32,16},{48,32},{64,48},{80,64},{96,80},{112,96},{17,1},{33... | collective-permute-start | bytes 1572872 | tf_op jit(solution)/shard_map/ppermute | solution.py:17
  312.8 27.4 %collective-permute-start.23 = (f32[16,8,64,16]{2,3,1,0:T(8,128)S(1)}, f32[16,8,64,16]{2,3,1,0:T(8,128)S(1)}, u32[]{:S(2)}, u32[]{:S(2)}) collective-permute-start(f32[16,8,64,16]{2,3,1,0:T(8,128)S(1)} %multiply_add_fusion.4), channel_id=1, source_target_pairs={{2,0},{4,2},{6,4},{8,6},{10,8},{12,10},{14,12},{3,1},{5,3},{7,5},{... | collective-permute-start | bytes 1572872 | tf_op jit(solution)/shard_map/ppermute | solution.py:17
  338.8 27.9 %collective-permute-start.16 = (f32[16,8,64,16]{2,3,1,0:T(8,128)S(1)}, f32[16,8,64,16]{2,3,1,0:T(8,128)S(1)}, u32[]{:S(2)}, u32[]{:S(2)}) collective-permute-start(f32[16,8,64,16]{2,3,1,0:T(8,128)S(1)} %multiply_add_fusion.10), channel_id=1, source_target_pairs={{16,0},{32,16},{48,32},{64,48},{80,64},{96,80},{112,96},{17,1},{33... | collective-permute-start | bytes 1572872 | tf_op jit(solution)/shard_map/ppermute | solution.py:17
  340.4 27.8 %collective-permute-start.24 = (f32[16,8,64,16]{2,3,1,0:T(8,128)S(1)}, f32[16,8,64,16]{2,3,1,0:T(8,128)S(1)}, u32[]{:S(2)}, u32[]{:S(2)}) collective-permute-start(f32[16,8,64,16]{2,3,1,0:T(8,128)S(1)} %multiply_add_fusion.3), channel_id=1, source_target_pairs={{2,0},{4,2},{6,4},{8,6},{10,8},{12,10},{14,12},{3,1},{5,3},{7,5},{... | collective-permute-start | bytes 1572872 | tf_op jit(solution)/shard_map/ppermute | solution.py:17
  366.9 26.8 %collective-permute-start.17 = (f32[16,8,64,16]{2,3,1,0:T(8,128)S(1)}, f32[16,8,64,16]{2,3,1,0:T(8,128)S(1)}, u32[]{:S(2)}, u32[]{:S(2)}) collective-permute-start(f32[16,8,64,16]{2,3,1,0:T(8,128)S(1)} %multiply_add_fusion.9), channel_id=1, source_target_pairs={{16,0},{32,16},{48,32},{64,48},{80,64},{96,80},{112,96},{17,1},{33... | collective-permute-start | bytes 1572872 | tf_op jit(solution)/shard_map/ppermute | solution.py:17
  368.4 27.0 %collective-permute-start.25 = (f32[16,8,64,16]{2,3,1,0:T(8,128)S(1)}, f32[16,8,64,16]{2,3,1,0:T(8,128)S(1)}, u32[]{:S(2)}, u32[]{:S(2)}) collective-permute-start(f32[16,8,64,16]{2,3,1,0:T(8,128)S(1)} %multiply_add_fusion.2), channel_id=1, source_target_pairs={{2,0},{4,2},{6,4},{8,6},{10,8},{12,10},{14,12},{3,1},{5,3},{7,5},{... | collective-permute-start | bytes 1572872 | tf_op jit(solution)/shard_map/ppermute | solution.py:17
  394.0 6.3 copy-start.33
  394.0 6.3 copy-start.71
  394.0 6.3 copy-start.72
  394.0 26.1 %collective-permute-start.18 = (f32[16,8,64,16]{2,3,1,0:T(8,128)S(1)}, f32[16,8,64,16]{2,3,1,0:T(8,128)S(1)}, u32[]{:S(2)}, u32[]{:S(2)}) collective-permute-start(f32[16,8,64,16]{2,3,1,0:T(8,128)S(1)} %multiply_add_fusion.8), channel_id=1, source_target_pairs={{16,0},{32,16},{48,32},{64,48},{80,64},{96,80},{112,96},{17,1},{33... | collective-permute-start | bytes 1572872 | tf_op jit(solution)/shard_map/ppermute | solution.py:17
  395.7 27.1 %collective-permute-start.26 = (f32[16,8,64,16]{2,3,1,0:T(8,128)S(1)}, f32[16,8,64,16]{2,3,1,0:T(8,128)S(1)}, u32[]{:S(2)}, u32[]{:S(2)}) collective-permute-start(f32[16,8,64,16]{2,3,1,0:T(8,128)S(1)} %multiply_add_fusion.1), channel_id=1, source_target_pairs={{2,0},{4,2},{6,4},{8,6},{10,8},{12,10},{14,12},{3,1},{5,3},{7,5},{... | collective-permute-start | bytes 1572872 | tf_op jit(solution)/shard_map/ppermute | solution.py:17
  421.4 8.3 %copy-start.37 = (f32[16,16,8]{2,0,1:T(8,128)S(1)}, f32[16,16,8]{2,0,1:T(8,128)}, u32[]{:S(2)}) copy-start(f32[16,16,8]{2,0,1:T(8,128)} %copy-done.35) | copy-start | bytes 24580
  421.4 8.3 %copy-start.80 = (f32[16,16,8]{2,0,1:T(8,128)S(1)}, f32[16,16,8]{2,0,1:T(8,128)}, u32[]{:S(2)}) copy-start(f32[16,16,8]{2,0,1:T(8,128)} %copy.307) | copy-start | bytes 24580
  421.4 8.4 %copy-start.81 = (f32[16,16,8]{2,0,1:T(8,128)S(1)}, f32[16,16,8]{2,0,1:T(8,128)}, u32[]{:S(2)}) copy-start(f32[16,16,8]{2,0,1:T(8,128)} %copy.308) | copy-start | bytes 24580
  421.4 8.4 %copy-start.82 = (f32[16,16,8]{2,0,1:T(8,128)S(1)}, f32[16,16,8]{2,0,1:T(8,128)}, u32[]{:S(2)}) copy-start(f32[16,16,8]{2,0,1:T(8,128)} %copy.309) | copy-start | bytes 24580
  421.4 25.5 %collective-permute-start.19 = (f32[16,8,64,16]{2,3,1,0:T(8,128)}, f32[16,8,64,16]{2,3,1,0:T(8,128)}, u32[]{:S(2)}, u32[]{:S(2)}) collective-permute-start(f32[16,8,64,16]{2,3,1,0:T(8,128)} %multiply_add_fusion.7), channel_id=1, source_target_pairs={{16,0},{32,16},{48,32},{64,48},{80,64},{96,80},{112,96},{17,1},{33... | collective-permute-start | bytes 1572872 | tf_op jit(solution)/shard_map/ppermute | solution.py:17
  424.0 6.7 copy-start.88
  424.0 27.0 %collective-permute-start.27 = (f32[16,8,64,16]{2,3,1,0:T(8,128)}, f32[16,8,64,16]{2,3,1,0:T(8,128)}, u32[]{:S(2)}, u32[]{:S(2)}) collective-permute-start(f32[16,8,64,16]{2,3,1,0:T(8,128)} %multiply_add_fusion), channel_id=1, source_target_pairs={{2,0},{4,2},{6,4},{8,6},{10,8},{12,10},{14,12},{3,1},{5,3},{7,5},{... | collective-permute-start | bytes 1572872 | tf_op jit(solution)/shard_map/ppermute | solution.py:17
  431.8 19.3 %copy-start.23 = (f32[16,8,64,16]{2,3,1,0:T(8,128)S(1)}, f32[16,8,64,16]{2,3,1,0:T(8,128)}, u32[]{:S(2)}) copy-start(f32[16,8,64,16]{2,3,1,0:T(8,128)} %copy-done.21) | copy-start | bytes 1572868
  449.4 24.4 %collective-permute-start.20 = (f32[16,8,64,16]{2,3,1,0:T(8,128)}, f32[16,8,64,16]{2,3,1,0:T(8,128)S(1)}, u32[]{:S(2)}, u32[]{:S(2)}) collective-permute-start(f32[16,8,64,16]{2,3,1,0:T(8,128)} %multiply_add_fusion.6), channel_id=1, source_target_pairs={{16,0},{32,16},{48,32},{64,48},{80,64},{96,80},{112,96},{17,1},{33... | collective-permute-start | bytes 1572872 | tf_op jit(solution)/shard_map/ppermute | solution.py:17
  460.8 15.0 %copy-start.9 = (f32[16,16,8,64]{3,0,2,1:T(8,128)S(1)}, f32[16,16,8,64]{3,0,2,1:T(8,128)}, u32[]{:S(2)}) copy-start(f32[16,16,8,64]{3,0,2,1:T(8,128)} %copy-done.6) | copy-start | bytes 1572868
  460.8 15.0 %copy-start.70 = (f32[16,16,16]{1,2,0:T(8,128)S(1)}, f32[16,16,16]{1,2,0:T(8,128)}, u32[]{:S(2)}) copy-start(f32[16,16,16]{1,2,0:T(8,128)} %copy.386) | copy-start | bytes 49156
  473.8 8.4 %copy-start.18 = (f32[16,8,64,16]{2,3,1,0:T(8,128)}, f32[16,8,64,16]{2,3,1,0:T(8,128)S(1)}, u32[]{:S(2)}) copy-start(f32[16,8,64,16]{2,3,1,0:T(8,128)S(1)} %collective-permute-done.20) | copy-start | bytes 1572868
  492.5 78.0 %copy-start.28 = (f32[1,16,16,8,64]{4,2,3,1,0:T(8,128)S(1)}, f32[1,16,16,8,64]{4,2,3,1,0:T(8,128)}, u32[]{:S(2)}) copy-start(f32[1,16,16,8,64]{4,2,3,1,0:T(8,128)} %get-tuple-element.82) | copy-start | bytes 1572868
  (80 other events, 151.1 us)
Sparse Core Ops, SparseCore 0:
  575.6 146.2 all-reduce.13
where the time goes:
time: 743 us; the launch traced here: 733 us
  waiting for transfers between devices  368 us (50%)
  starting transfers between devices  118 us (16%)
  blocking collectives  73.7 us (10%)
  matrix products  65.6 us (9%)
  other arithmetic  51.3 us (7%)
  local copies, waits for them, and re-layouts  39.5 us (5%)
  between operations  16.3 us (2%)
    ppermute x28, waiting for transfers between devices, from_behind(): return lax.ppermute(block, axis, route)  224 us
    psum x1, waiting for transfers between devices, local(): lax.psum((outer_sum(tokens, d_proj), outer_sum(tokens, d_ssm), outer_sum(...  144 us
    ppermute x28, starting transfers between devices, from_behind(): return lax.ppermute(block, axis, route)  118 us
    psum x1, blocking collectives, local(): lax.psum((outer_sum(tokens, d_proj), outer_sum(tokens, d_ssm), outer_sum(...  73.7 us
    dot_general x6, matrix products, block_terms(): jnp.einsum('sjh,sjn,sjhp->shpn', weight, in_map, drive, precision=highest)  22.8 us
    unnamed x232, local copies, waits for them, and re-layouts  19.6 us
    dot_general x6, matrix products, block_out(): jnp.einsum('sijh,sij,sjhp->sihp', decay_mask, scores, drive, precision=hi...  19.3 us
  transfers between devices with their start and end apart: 29, of which 17 were waited for; matrix products, arithmetic and copies ran while one was open for 8% of the time, Pallas kernels for 0%

commit v1 on v0

v1 whole, which is shorter than its diff:
```python
import functools

import jax
import jax.numpy as jnp
from jax import lax
from jax.experimental import pallas as pl
from jax.experimental.pallas import tpu as pltpu
from jax.sharding import PartitionSpec as P

MESH = pl.DeviceIdType.MESH
F32 = jnp.float32
BF16 = jnp.bfloat16
HEADS = 8
HDIM = 64
STATE = 16
SIDE = 16
T = SIDE * SIDE
E = HEADS * HDIM
D = 256
CH = 4
CR = 128 // CH
NEG = -1e30
EARLY = 2048
LATE = 1280


def mm(a, b, ca=1, cb=0):
    return lax.dot_general(a, b, (((ca,), (cb,)), ((), ())), preferred_element_type=F32)


def split(x, terms):
    out = []
    for _ in range(terms - 1):
        hi = x.astype(BF16)
        out.append(hi)
        x = x - hi.astype(F32)
    out.append(x.astype(BF16))
    return out


def pick(mask, x, terms=3):
    return functools.reduce(lambda u, v: u + v, [mm(mask, part) for part in split(x, terms)])


def spread(x, mask, terms=2):
    return functools.reduce(lambda u, v: u + v, [mm(part, mask) for part in split(x, terms)])


def mm3(a, b, ca=1, cb=0):
    (ah, al), (bh, bl) = a, b
    return mm(ah, bh, ca, cb) + (mm(ah, bl, ca, cb) + mm(al, bh, ca, cb))


def keep(pair, where, x):
    hi, lo = split(x, 2)
    pair[(0,) + where] = hi
    pair[(1,) + where] = lo


def both(pair):
    return pair[0], pair[1]


def only(mask, pair):
    nil = jnp.zeros(mask.shape, BF16)
    return jnp.where(mask, pair[0], nil), jnp.where(mask, pair[1], nil)


def ind(cond):
    return jnp.where(cond, 1.0, 0.0).astype(BF16)


def grid2(rows, cols):
    return (
        lax.broadcasted_iota(jnp.int32, (rows, cols), 0),
        lax.broadcasted_iota(jnp.int32, (rows, cols), 1),
    )


def hi4(x):
    return lax.shift_right_logical(x, 4)


def lo4(x):
    return jnp.bitwise_and(x, 15)


def head_spread():
    r, c = grid2(128, E)
    return ind(r == lax.shift_right_logical(c, 6))


def head_sum(x):
    r, c = grid2(E, 128)
    return spread(x, ind(lax.shift_right_logical(r, 6) == c), 2)


def place():
    row, col, slide = lax.axis_index("row"), lax.axis_index("col"), lax.axis_index("slide")
    return dict(y=row // 2, xh=lax.rem(row, 2), z=col // 2, co=lax.rem(col, 2), xl=slide)


def at(pos, **change):
    p = dict(pos, **change)
    return (p["y"] * 2 + p["xh"], p["z"] * 2 + p["co"], p["xl"])


def flip(bit, by):
    return bit + by * (1 - 2 * bit)


def peers(pos, axis):
    out = []
    for d in (1, 2, 3):
        if axis == "x":
            out.append(at(pos, xh=flip(pos["xh"], d // 2), xl=flip(pos["xl"], d % 2)))
        else:
            out.append(at(pos, **{axis: xor4(pos[axis], d)}))
    return out


def xor4(q, d):
    return 2 * flip(q // 2, d // 2) + flip(lax.rem(q, 2), d % 2)


def remote(src, dst, ssem, rsem, to):
    return pltpu.make_async_remote_copy(
        src_ref=src, dst_ref=dst, send_sem=ssem, recv_sem=rsem, device_id=to, device_id_type=MESH
    )


class Chain:
    def __init__(self, pos, axis, back, own, got, into, send, ret, res, dec, deco, ssem, rsem, slot):
        self.bit, step = ("co", "z") if axis == "r" else ("xh", "y")
        b, q = pos[self.bit], pos[step]
        self.b = b
        self.first = (b == 1) if back else (b == 0)
        self.r = (3 - q) if back else q
        self.nxt = at(pos, **{step: lax.rem(q + (3 if back else 1), 4)})
        self.partner = at(pos, **{self.bit: 1 - b})
        self.own, self.got, self.into, self.send, self.ret, self.res = own, got, into, send, ret, res
        self.dec, self.deco = dec, deco
        self.ssem, self.rsem, self.slot = ssem, rsem, slot

    def half(self, mine, c):
        start = (self.b if mine else 1 - self.b) * 128 + c * CR
        return pl.ds(pl.multiple_of(start, CR), CR)

    def sems(self, stage, c):
        return self.ssem.at[self.slot, stage, c], self.rsem.at[self.slot, stage, c]

    def c_exch(self, c):
        return remote(self.own.at[self.half(False, c)], self.got.at[pl.ds(c * CR, CR)], *self.sems(0, c), self.partner)

    def c_hop(self, c):
        return remote(self.send.at[pl.ds(c * CR, CR)], self.into.at[pl.ds(c * CR, CR)], *self.sems(1, c), self.nxt)

    def c_ret(self, c):
        return remote(self.ret.at[pl.ds(c * CR, CR)], self.res.at[self.half(True, c)], *self.sems(2, c), self.partner)

    def start(self):
        @pl.when(self.r == 0)
        def _():
            self.into[...] = jnp.zeros((128, E), F32)

        for c in range(CH):
            self.c_exch(c).start()

    def pair(self, c):
        sl = pl.ds(c * CR, CR)
        self.c_exch(c).wait_recv()
        got, own = self.got[sl], self.own[self.half(True, c)]
        d_own, d_oth = self.dec[self.half(True, c)], self.deco[sl]
        lead = jnp.where(self.first, own, got)
        tail = jnp.where(self.first, got, own)
        d_tail = jnp.where(self.first, d_oth, d_own)
        self.send[sl] = tail + d_tail * lead

        @pl.when(self.r == 0)
        def _():
            self.c_hop(c).start()

    def hop(self, c):
        sl = pl.ds(c * CR, CR)

        @pl.when(self.r > 0)
        def _():
            self.c_hop(c).wait_recv()

        enter = self.into[sl]
        d_own, d_oth = self.dec[self.half(True, c)], self.deco[sl]

        @pl.when((self.r > 0) & (self.r < 3))
        def _():
            self.send[sl] = self.send[sl] + d_own * d_oth * enter
            self.c_hop(c).start()

        lead = jnp.where(self.first, self.own[self.half(True, c)], self.got[sl])
        d_lead = jnp.where(self.first, d_own, d_oth)
        after = d_lead * enter + lead
        self.ret[sl] = jnp.where(self.first, after, enter)
        self.c_ret(c).start()
        self.res[self.half(True, c)] = jnp.where(self.first, enter, after)

    def finish(self):
        for c in range(CH):
            self.c_ret(c).wait_recv()

    def drain(self):
        for c in range(CH):
            self.c_exch(c).wait_send()
            self.c_ret(c).wait_send()

            @pl.when(self.r < 3)
            def _():
                self.c_hop(c).wait_send()


def run_hops(a, c):
    @pl.when(a.r <= c.r)
    def _():
        for who, at_chunk in ((a, 0), (a, 1), (c, 0), (a, 2), (c, 1), (a, 3), (c, 2), (c, 3)):
            who.hop(at_chunk)

    @pl.when(a.r > c.r)
    def _():
        for who, at_chunk in ((c, 0), (c, 1), (a, 0), (c, 2), (a, 1), (c, 3), (a, 2), (a, 3)):
            who.hop(at_chunk)


class Total:
    def __init__(self, pos, buf, out, cbuf, xbuf, ybuf, zbuf, ssem, rsem):
        n = buf.shape[0]
        self.pos, self.buf, self.out = pos, buf, out
        self.cbuf, self.xbuf, self.ybuf, self.zbuf = cbuf, xbuf, ybuf, zbuf
        self.ssem, self.rsem = ssem, rsem
        self.nh = n // 2
        self.base = pos["co"] * self.nh
        self.other = at(pos, co=1 - pos["co"])
        index = {"x": pos["xh"] * 2 + pos["xl"], "y": pos["y"], "z": pos["z"]}
        third = -(-self.nh // 384) * 128
        sizes = (third, third, self.nh - 2 * third)
        self.parts, offset = [], 0
        for size, order in zip(sizes, ("xyz", "yzx", "zxy")):
            start = self.base + offset
            first = start + index[order[0]] * (size // 4)
            second = first + index[order[1]] * (size // 16)
            self.parts.append((order, index[order[0]], index[order[1]], size, offset, start, first, second))
            offset += size

    def rows(self, start, size):
        return pl.ds(pl.multiple_of(start, 8), size)

    def copies(self, stage):
        pos = self.pos
        if stage in (0, 6):
            src = self.buf.at[self.rows((1 - pos["co"]) * self.nh, self.nh)]
            own = self.out.at[self.rows(self.base, self.nh)]
            src, dst = (src, self.cbuf) if stage == 0 else (own, own)
            return [remote(src, dst, self.ssem.at[stage, 0], self.rsem.at[stage, 0], self.other)]
        out = []
        for p, (order, g0, g1, size, offset, start, first, second) in enumerate(self.parts):
            n0, n1 = size // 4, size // 16
            axis = order[(0, 1, 2, 1, 0)[stage - 1]]
            for d, to in enumerate(peers(pos, axis)):
                if stage == 1:
                    src = self.buf.at[self.rows(start + xor4(g0, d + 1) * n0, n0)]
                    dst = self.xbuf.at[d, pl.ds(offset // 4, n0)]
                elif stage == 2:
                    src = self.buf.at[self.rows(first + xor4(g1, d + 1) * n1, n1)]
                    dst = self.ybuf.at[d, pl.ds(offset // 16, n1)]
                elif stage == 3:
                    src, dst = self.buf.at[self.rows(second, n1)], self.zbuf.at[d, pl.ds(offset // 16, n1)]
                elif stage == 4:
                    src = dst = self.out.at[self.rows(second, n1)]
                else:
                    src = dst = self.out.at[self.rows(first, n0)]
                k = 3 * p + d
                out.append(remote(src, dst, self.ssem.at[stage, k], self.rsem.at[stage, k], to))
        return out

    def start(self, stage):
        for copy in self.copies(stage):
            copy.start()

    def finish(self, stage):
        for copy in self.copies(stage):
            copy.wait()
        if stage == 0:
            sl = self.rows(self.base, self.nh)
            self.buf[sl] = self.buf[sl] + self.cbuf[...]
        if stage not in (1, 2, 3):
            return
        came = (self.xbuf, self.ybuf, self.zbuf)[stage - 1]
        to = self.out if stage == 3 else self.buf
        for order, g0, g1, size, offset, start, first, second in self.parts:
            share = 4 if stage == 1 else 16
            sl = self.rows(first if stage == 1 else second, size // share)
            at_ = pl.ds(offset // share, size // share)
            to[sl] = (self.buf[sl] + came[0, at_]) + (came[1, at_] + came[2, at_])

    def step(self, stage):
        self.finish(stage)
        if stage < 6:
            self.start(stage + 1)


def kernel(factor, *refs):
    names_in = ["tok", "cot", "wi", "ws", "bias", "rate", "skip", "gain", "wo"]
    names_out = ["lo", "gt", "eres", "lres"]
    n_io = len(names_in) + len(names_out)
    k = dict(zip(names_in + names_out, refs[:n_io]))
    k.update(zip([name for name, _ in SCRATCH], refs[n_io:]))
    body(factor, **k)


def vm(*shape, dtype=F32):
    return pltpu.VMEM(shape, dtype)


BIG = (T, E)
SCRATCH = [
    ("x", vm(*BIG)), ("z", vm(*BIG)), ("ub", vm(2, *BIG, dtype=BF16)), ("stepe", vm(*BIG)),
    ("bt", vm(2, T, T, dtype=BF16)), ("ct", vm(2, T, T, dtype=BF16)), ("s", vm(T, T)), ("ds", vm(T, T)),
    ("wsel", vm(D, 640, dtype=BF16)), ("wpad", vm(D, 128, dtype=BF16)), ("vecs", vm(8, 128)),
    ("step", vm(T, 128)), ("sig", vm(T, 128)),
    ("cumr", vm(T, 128)), ("cumc", vm(T, 128)), ("cumrt", vm(128, T)), ("cumct", vm(128, T)),
    ("er", vm(*BIG)), ("ec", vm(*BIG)), ("wr", vm(*BIG)), ("wc", vm(*BIG)), ("dr", vm(*BIG)), ("dc", vm(*BIG)),
    ("dro", vm(128, E)), ("dco", vm(128, E)),
    ("finr", vm(SIDE, 128)), ("finc", vm(SIDE, 128)), ("finro", vm(SIDE, 128)), ("finco", vm(SIDE, 128)),
    ("wur", vm(2, *BIG, dtype=BF16)), ("wuc", vm(2, *BIG, dtype=BF16)),
    ("edr", vm(2, *BIG, dtype=BF16)), ("edc", vm(2, *BIG, dtype=BF16)),
    ("mr", vm(2, HEADS, T, T, dtype=BF16)), ("mc", vm(2, HEADS, T, T, dtype=BF16)), ("ls", vm(HEADS, T, T)),
    ("yr", vm(*BIG)), ("yc", vm(*BIG)), ("car", vm(*BIG)), ("cac", vm(*BIG)), ("dn", vm(*BIG)),
    ("dy", vm(*BIG)), ("dyb", vm(2, *BIG, dtype=BF16)), ("dzb", vm(*BIG, dtype=BF16)), ("nb", vm(*BIG, dtype=BF16)),
    ("qr", vm(*BIG)), ("qc", vm(*BIG)), ("dxb", vm(*BIG, dtype=BF16)), ("dux", vm(*BIG)),
    ("dbe", vm(T, T)), ("dce", vm(T, T)),
    ("own", pltpu.VMEM((4, T, E), F32)), ("got", pltpu.VMEM((4, 128, E), F32)), ("into", pltpu.VMEM((4, 128, E), F32)),
    ("send", pltpu.VMEM((4, 128, E), F32)), ("ret", pltpu.VMEM((4, 128, E), F32)), ("res", pltpu.VMEM((4, T, E), F32)),
    ("ebuf", vm(EARLY, 128)), ("ecb", vm(EARLY // 2, 128)), ("exb", vm(3, EARLY // 8, 128)),
    ("eyb", vm(3, EARLY // 32, 128)), ("ezb", vm(3, EARLY // 32, 128)),
    ("lbuf", vm(LATE, 128)), ("lcb", vm(LATE // 2, 128)), ("lxb", vm(3, LATE // 8, 128)),
    ("lyb", vm(3, LATE // 32, 128)), ("lzb", vm(3, LATE // 32, 128)),
    ("fsem", pltpu.SemaphoreType.DMA((2, 2))),
    ("cs", pltpu.SemaphoreType.DMA((4, 3, CH))), ("cr", pltpu.SemaphoreType.DMA((4, 3, CH))),
    ("es", pltpu.SemaphoreType.DMA((7, 9))), ("erv", pltpu.SemaphoreType.DMA((7, 9))),
    ("lsm", pltpu.SemaphoreType.DMA((7, 9))), ("lrv", pltpu.SemaphoreType.DMA((7, 9))),
]
RB = 32


def loop(rows, fn, init=0):
    def step(i, carry):
        return fn(pl.ds(pl.multiple_of(i * RB, RB), RB), i, carry)

    return lax.fori_loop(0, rows // RB, step, init)


def body(factor, tok, cot, wi, ws, bias, rate, skip, gain, wo, lo, gt, eres, lres,
         x, z, ub, stepe, bt, ct, s, ds, wsel, wpad, vecs, step, sig, cumr, cumc, cumrt, cumct,
         er, ec, wr, wc, dr, dc, dro, dco, finr, finc, finro, finco, wur, wuc, edr, edc, mr, mc, ls,
         yr, yc, car, cac, dn, dy, dyb, dzb, nb, qr, qc, dxb, dux, dbe, dce,
         own, got, into, send, ret, res, ebuf, ecb, exb, eyb, ezb, lbuf, lcb, lxb, lyb, lzb,
         fsem, cs, cr, es, erv, lsm, lrv):
    pos = place()
    barrier = pltpu.get_barrier_semaphore()
    near = [at(pos, co=1 - pos["co"])] + peers(pos, "x") + peers(pos, "y") + peers(pos, "z")
    for to in near:
        pl.semaphore_signal(barrier, inc=1, device_id=to, device_id_type=MESH)

    def chain(slot, axis, back):
        a = slot % 2
        return Chain(pos, axis, back, own.at[slot], got.at[slot], into.at[slot], send.at[slot], ret.at[slot],
                     res.at[slot], (dr, dc)[a], (dro, dco)[a], cs, cr, slot)

    fr, fc, gr_, gc_ = chain(0, "r", False), chain(1, "c", False), chain(2, "r", True), chain(3, "c", True)
    early = Total(pos, ebuf, eres, ecb, exb, eyb, ezb, es, erv)
    late = Total(pos, lbuf, lres, lcb, lxb, lyb, lzb, lsm, lrv)

    r, c = grid2(2 * STATE + HEADS, 640)
    sel = ((c < 256) & (r == lo4(c))) | ((c >= 256) & (c < 512) & (r == 16 + lo4(c))) | ((c >= 512) & (r == c - 480))
    wsel[...] = mm(ws[...], ind(sel), 0, 0).astype(BF16)
    r, c = grid2(2 * STATE + HEADS, 128)
    wpad[...] = mm(ws[...], ind(r == c), 0, 0).astype(BF16)
    vecs[...] = jnp.zeros((8, 128), F32)
    vecs[0:1, 0:HEADS] = bias[...]
    vecs[1:2, 0:HEADS] = rate[...]
    vecs[2:3, 0:HEADS] = skip[...]
    raw = mm(tok[...], wsel[:, 512:640]) + vecs[0:1, :]
    tail = jnp.exp(-jnp.abs(raw))
    stp = jnp.maximum(raw, 0.0) + jnp.log1p(tail)
    step[...] = stp
    sig[...] = jnp.where(raw >= 0, 1.0, tail) / (1.0 + tail)
    a = -stp * vecs[1:2, :]
    t, u = grid2(T, T)
    same_r, same_c = hi4(t) == hi4(u), lo4(t) == lo4(u)
    cumr[...] = pick(ind(same_r & (u <= t)), a)
    cumc[...] = pick(ind(same_c & (u <= t)), a)
    aft_r = pick(ind(same_r & (u > t)), a)
    aft_c = pick(ind(same_c & (u > t)), a)
    r, c = grid2(SIDE, T)
    finr[...] = jnp.exp(pick(ind(r == hi4(c)), a))
    finc[...] = jnp.exp(pick(ind(r == lo4(c)), a))
    hx = head_spread()
    stepe[...] = spread(stp, hx, 3)
    wr[...] = spread(jnp.exp(aft_r), hx)
    wc[...] = spread(jnp.exp(aft_c), hx)
    x[...] = mm(tok[...], wi[:, 0:E])
    keep(bt, (), mm(tok[...], wsel[:, 0:256]))

    def drive(sl, i, carry):
        u_ = stepe[sl] * x[sl]
        keep(ub, (sl,), u_)
        keep(wur, (sl,), wr[sl] * u_)
        keep(wuc, (sl,), wc[sl] * u_)
        return carry

    loop(T, drive)
    line_r, line_c = hi4(t) == hi4(u), lo4(t) == hi4(u)
    own[1] = mm3(only(line_c, bt), both(wuc), 0, 0)
    own[0] = mm3(only(line_r, bt), both(wur), 0, 0)
    pl.semaphore_wait(barrier, len(near))
    f_r = remote(finr, finro, fsem.at[0, 0], fsem.at[0, 1], fr.partner)
    f_c = remote(finc, finco, fsem.at[1, 0], fsem.at[1, 1], fc.partner)
    f_r.start()
    f_c.start()
    fr.start()
    fc.start()

    def lines(rows, first, ends):
        k, l = grid2(rows, SIDE)
        return pick(ind(hi4(k) + first == l), spread(ends, hx), 2)

    dr[...] = lines(T, 0, finr[...])
    dc[...] = lines(T, 0, finc[...])
    f_r.wait_recv()
    dro[...] = lines(128, pos["co"] * 8, finro[...])
    for q in range(CH):
        fr.pair(q)

    z[...] = mm(tok[...], wi[:, E : 2 * E])
    keep(ct, (), mm(tok[...], wsel[:, 256:512]))
    s[...] = mm3(both(ct), both(bt), 1, 1) * (1.0 / 16.0)
    er[...] = spread(jnp.exp(cumr[...]), hx)
    ec[...] = spread(jnp.exp(cumc[...]), hx)
    cumrt[...] = cumr[...].T
    cumct[...] = cumc[...].T

    def masks(sl, i, carry):
        t_, u_ = grid2(RB, T)
        t_ = t_ + i * RB
        in_r = (hi4(t_) == hi4(u_)) & (u_ <= t_)
        in_c = (lo4(t_) == lo4(u_)) & (u_ <= t_)
        s_ = s[sl]
        c_r, c_c = cumr[sl], cumc[sl]
        for h in range(HEADS):
            l_r = jnp.exp(jnp.where(in_r, c_r[:, h : h + 1] - cumrt[h : h + 1, :], NEG))
            l_c = jnp.exp(jnp.where(in_c, c_c[:, h : h + 1] - cumct[h : h + 1, :], NEG))
            keep(mr, (h, sl), l_r * s_)
            keep(mc, (h, sl), l_c * s_)
            ls[h, sl] = l_r + l_c
        return carry

    loop(T, masks)
    f_c.wait_recv()
    dco[...] = lines(128, pos["xh"] * 8, finco[...])
    for q in range(CH):
        fc.pair(q)
    low = lax.broadcasted_iota(jnp.int32, (T, 128), 1) < HDIM

    def heads(m, hp, pair, dim):
        wide = jnp.concatenate(pair, axis=1)
        part = []
        for h in (2 * hp, 2 * hp + 1):
            full = mm(m[0, h], wide, dim, 0)
            part.append(full[:, :128] + full[:, 128:] + mm(m[1, h], pair[0], dim, 0))
        return jnp.where(low, part[0], part[1])

    def within(hp, carry):
        sl = pl.ds(pl.multiple_of(hp * 128, 128), 128)
        u_ = (ub[0, :, sl], ub[1, :, sl])
        yr[:, sl] = heads(mr, hp, u_, 1)
        yc[:, sl] = heads(mc, hp, u_, 1)
        return carry

    lax.fori_loop(0, HEADS // 2, within, 0)
    dn[...] = mm(cot[...], wo[...], 1, 1)
    run_hops(fr, fc)
    fr.finish()
    car[...] = mm3(only(line_r, ct), split(res[0], 2))
    fc.finish()
    cac[...] = mm3(only(line_c, ct), split(res[1], 2))

    skipe = spread(vecs[...], hx, 3)[2:3, :]
    gain_ = gain[...]

    def middle(sl, i, carry):
        sum_gain, sum_skip = carry
        x_, z_ = x[sl], z[sl]
        c_r, c_c = er[sl] * car[sl], ec[sl] * cac[sl]
        w_r, w_c = yr[sl], yc[sl]
        y = (w_r + w_c) + (c_r + c_c) + skipe * x_
        sg = 1.0 / (1.0 + jnp.exp(-z_))
        act = z_ * sg
        gated = y * act
        inv = lax.rsqrt(jnp.mean(gated * gated, axis=-1, keepdims=True) + 1e-05)
        unit = gated * inv
        nb[sl] = (unit * gain_).astype(BF16)
        d_n = dn[sl]
        g1 = d_n * gain_
        dg = inv * (g1 - unit * jnp.mean(g1 * unit, axis=-1, keepdims=True))
        d_y = dg * act
        dzb[sl] = (dg * y * (sg * (1.0 + z_ * (1.0 - sg)))).astype(BF16)
        dy[sl] = d_y
        keep(dyb, (sl,), d_y)
        keep(edr, (sl,), er[sl] * d_y)
        keep(edc, (sl,), ec[sl] * d_y)
        qr[sl] = d_y * (c_r + w_r)
        qc[sl] = d_y * (c_c + w_c)
        fold = lambda v: functools.reduce(lambda p, q: p + q, [v[8 * j : 8 * j + 8] for j in range(RB // 8)])
        return sum_gain + fold(d_n * unit), sum_skip + fold(d_y * x_)

    nil = jnp.zeros((8, E), F32)
    sum_gain, sum_skip = loop(T, middle, (nil, nil))
    own[3] = mm3(only(line_c, ct), both(edc), 0, 0)
    gc_.start()
    own[2] = mm3(only(line_r, ct), both(edr), 0, 0)
    gr_.start()

    lg = mm(tok[...], dzb[...], 0, 0) * factor
    for j in range(4):
        ebuf[j * 256 : (j + 1) * 256] = lg[:, j * 128 : (j + 1) * 128]
    lg = mm(nb[...], cot[...], 0, 0) * factor
    for j in range(2):
        ebuf[1024 + j * 512 : 1024 + (j + 1) * 512] = lg[:, j * 128 : (j + 1) * 128]
    early.start(0)
    for q in range(CH):
        gr_.pair(q)
    early.step(0)

    def within_back(hp, carry):
        sl = pl.ds(pl.multiple_of(hp * 128, 128), 128)
        d_ = (dyb[0, :, sl], dyb[1, :, sl])
        yr[:, sl] = heads(mr, hp, d_, 0)
        yc[:, sl] = heads(mc, hp, d_, 0)
        return carry

    lax.fori_loop(0, HEADS // 2, within_back, 0)
    for q in range(CH):
        gc_.pair(q)
    ds[...] = jnp.zeros((T, T), F32)

    def scores_back(hp, carry):
        sl = pl.ds(pl.multiple_of(hp * 128, 128), 128)
        u_h, u_l = ub[0, :, sl], ub[1, :, sl]
        twice = jnp.concatenate((u_h, u_h), axis=1)
        total = ds[...]
        for j in (0, 1):
            d_h, d_l = only(low if j == 0 else ~low, (dyb[0, :, sl], dyb[1, :, sl]))
            pairs = mm(jnp.concatenate((d_h, d_l), axis=1), twice, 1, 1) + mm(d_h, u_l, 1, 1)
            total = total + ls[2 * hp + j] * pairs
        ds[...] = total
        return carry

    lax.fori_loop(0, HEADS // 2, scores_back, 0)
    head = u < STATE
    d_s = split(ds[...], 2)
    dce[...] = (
        jnp.where(line_r, mm3(both(edr), split(res[0], 2), 1, 1), 0.0)
        + jnp.where(line_c, mm3(both(edc), split(res[1], 2), 1, 1), 0.0)
        + jnp.where(head, mm3(d_s, both(bt)), 0.0)
    )
    dbe[...] = jnp.where(head, mm3(d_s, both(ct), 0, 0), 0.0)
    lo[...] = mm(nb[...], wo[...]).astype(BF16)
    run_hops(gr_, gc_)
    early.step(1)
    gr_.finish()
    g_r = split(res[2], 2)
    car[...] = mm3(only(line_r, bt), g_r)
    dbe[...] = dbe[...] + jnp.where(line_r, mm3(both(wur), g_r, 1, 1), 0.0)
    early.step(2)
    gc_.finish()
    g_c = split(res[3], 2)
    cac[...] = mm3(only(line_c, bt), g_c)
    dbe[...] = dbe[...] + jnp.where(line_c, mm3(both(wuc), g_c, 1, 1), 0.0)

    def last(sl, i, carry):
        x_, se = x[sl], stepe[sl]
        u_ = se * x_
        v_r, v_c = wr[sl] * car[sl], wc[sl] * cac[sl]
        w_r, w_c = yr[sl], yc[sl]
        qr[sl] = qr[sl] - u_ * (v_r + w_r)
        qc[sl] = qc[sl] - u_ * (v_c + w_c)
        d_u = (w_r + w_c) + (v_r + v_c)
        dux[sl] = d_u * x_
        dxb[sl] = (se * d_u + skipe * dy[sl]).astype(BF16)
        res[0, sl] = res[2, sl] * (own[0, sl] + dr[sl] * res[0, sl])
        res[1, sl] = res[3, sl] * (own[1, sl] + dc[sl] * res[1, sl])
        return carry

    loop(T, last)
    lg = mm(tok[...], dxb[...], 0, 0) * factor
    for j in range(4):
        lbuf[j * 256 : (j + 1) * 256] = lg[:, j * 128 : (j + 1) * 128]
    d_a = (
        pick(ind(same_r & (u >= t)), head_sum(qr[...]))
        + pick(ind(same_c & (u >= t)), head_sum(qc[...]))
        + pick(ind(line_r), head_sum(res[0]))
        + pick(ind(line_c), head_sum(res[1]))
    )
    d_step = head_sum(dux[...]) - vecs[1:2, :] * d_a
    d_raw = d_step * sig[...]
    r, c = grid2(T, 128)
    d_ssm = (
        spread(dbe[...], ind(c == lo4(r)))
        + spread(dce[...], ind(c == 16 + lo4(r)))
        + spread(d_raw, ind(grid2(128, 128)[1] == 32 + grid2(128, 128)[0]), 3)
    )
    d_ssm = d_ssm.astype(BF16)
    lg = mm(d_ssm, tok[...], 0, 0) * factor
    for j in range(2):
        lbuf[1024 + j * 128 : 1152 + j * 128] = lg[:, j * 128 : (j + 1) * 128]
    total_of = lambda v: jnp.sum(v, axis=0, keepdims=True)
    sum_gain = total_of(sum_gain) * factor
    for j in range(4):
        lbuf[1088 + j : 1089 + j] = sum_gain[:, j * 128 : (j + 1) * 128]
    lbuf[1092:1093] = total_of(d_raw) * factor
    lbuf[1093:1094] = -total_of(step[...] * d_a) * factor
    lbuf[1094:1095] = total_of(head_sum(sum_skip)) * factor
    late.start(0)
    early.step(3)
    late.step(0)
    back = mm(dxb[...], wi[:, 0:E], 1, 1) + mm(dzb[...], wi[:, E : 2 * E], 1, 1)
    back = back + mm(d_ssm, wpad[...], 1, 1)
    gt[...] = back.astype(BF16)
    early.step(4)
    late.step(1)
    early.step(5)
    late.step(2)
    early.step(6)
    late.step(3)
    for who in (fr, fc, gr_, gc_):
        who.drain()
    f_r.wait_send()
    f_c.wait_send()
    late.step(4)
    late.step(5)
    late.step(6)


def unpack(eres, lres, lo_in, gt_in, lo, gt, gi, gs, go, gb, gr, gk, gg):
    lo[...] = lo_in[...]
    gt[...] = gt_in[...]
    for j in range(4):
        gi[:, j * 128 : (j + 1) * 128] = lres[j * 256 : (j + 1) * 256]
        gi[:, E + j * 128 : E + (j + 1) * 128] = eres[j * 256 : (j + 1) * 256]
        gg[:, j * 128 : (j + 1) * 128] = lres[1088 + j : 1089 + j]
    for j in range(2):
        go[:, j * 128 : (j + 1) * 128] = eres[1024 + j * 512 : 1024 + (j + 1) * 512]
        gs[:, j * 128 : (j + 1) * 128] = lres[1024 + j * 128 : 1064 + j * 128]
    gb[...] = lres[1092:1093, 0:HEADS]
    gr[...] = lres[1093:1094, 0:HEADS]
    gk[...] = lres[1094:1095, 0:HEADS]


def local(tokens_in, out_cotangent, w_inner, w_ssm, dt_bias, decay_rate, skip_gain, norm_gain, w_out):
    devices = lax.axis_size("slide") * lax.axis_size("row") * lax.axis_size("col")
    factor = float(devices * T) ** -0.5
    shape = jax.ShapeDtypeStruct
    vmem = pl.BlockSpec(memory_space=pltpu.VMEM)
    lo, gt, eres, lres = pl.pallas_call(
        functools.partial(kernel, factor),
        out_shape=(shape((T, D), BF16), shape((T, D), BF16), shape((EARLY, 128), F32), shape((LATE, 128), F32)),
        in_specs=[vmem] * 9,
        out_specs=(vmem,) * 4,
        scratch_shapes=[kind for _, kind in SCRATCH],
        compiler_params=pltpu.CompilerParams(
            collective_id=0, has_side_effects=True, vmem_limit_bytes=48 * 2**20
        ),
    )(
        tokens_in.reshape(T, D),
        out_cotangent.reshape(T, D),
        w_inner,
        w_ssm.T,
        dt_bias.reshape(1, -1),
        decay_rate.reshape(1, -1),
        skip_gain.reshape(1, -1),
        norm_gain.reshape(1, -1),
        w_out,
    )
    out = pl.pallas_call(
        unpack,
        out_shape=(
            shape((T, D), BF16),
            shape((T, D), BF16),
            shape(w_inner.shape, F32),
            shape(w_ssm.shape[::-1], F32),
            shape(w_out.shape, F32),
            shape((1, HEADS), F32),
            shape((1, HEADS), F32),
            shape((1, HEADS), F32),
            shape((1, E), F32),
        ),
        in_specs=[vmem] * 4,
        out_specs=(vmem,) * 9,
        compiler_params=pltpu.CompilerParams(vmem_limit_bytes=6 * 2**20),
    )(eres, lres, lo, gt)
    return (
        out[0].reshape(tokens_in.shape),
        out[1].reshape(tokens_in.shape),
        out[2],
        out[3].T,
        out[4],
        out[5].reshape(-1),
        out[6].reshape(-1),
        out[7].reshape(-1),
        out[8].reshape(-1),
    )


def solution(mesh):
    tiles = P("slide", "row", "col", None)
    return jax.shard_map(
        local,
        mesh=mesh,
        in_specs=(tiles, tiles) + (P(),) * 7,
        out_specs=(tiles, tiles) + (P(),) * 7,
        check_vma=False,
    )
```

time: 743 us -> 102 us (0.14); the launches traced: 733 us -> 102 us
  waiting for transfers between devices: 368 us -> 0 us
  starting transfers between devices: 118 us -> 0 us
  Pallas kernels: 0 us -> 95.7 us
  blocking collectives: 73.7 us -> 0 us
  matrix products: 65.6 us -> 0 us
  other arithmetic: 51.3 us -> 0 us
  local copies, waits for them, and re-layouts: 39.5 us -> 5.2 us
  between operations: 16.3 us -> 0.69 us
    ppermute x28 -> x0, waiting for transfers between devices: 224 us -> none  [from_behind(): return lax.ppermute(block, axis, route)]
    psum x1 -> x0, waiting for transfers between devices: 144 us -> none  [local(): lax.psum((outer_sum(tokens, d_proj), outer_sum(tokens, d_ssm), outer_sum(...]
    ppermute x28 -> x0, starting transfers between devices: 118 us -> none  [from_behind(): return lax.ppermute(block, axis, route)]
    pallas_call x0 -> x2, Pallas kernels: none -> 95.7 us  [the longest x1 94.3 us: local(): pl.pallas_call(functools.partial(kernel, factor), out_shape=(shape((T, D)...]
    psum x1 -> x0, blocking collectives: 73.7 us -> none  [local(): lax.psum((outer_sum(tokens, d_proj), outer_sum(tokens, d_ssm), outer_sum(...]
    dot_general x33 -> x0, matrix products: 65.6 us -> none  [the longest x6 22.8 us: block_terms(): jnp.einsum('sjh,sjn,sjhp->shpn', weight, in_map, drive, precision=highest)]
    reduce_sum x10 -> x0, other arithmetic: 20.6 us -> none  [the longest x2 12.8 us: block_out(): return within + jnp.exp(cumulative)[..., None] * carried]
    add x26 -> x0, other arithmetic: 16.5 us -> none  [the longest x6 4.73 us: local(): decay_col[..., None, None] * in_col + fresh_col]
  transfers between devices with their start and end apart: 29 -> 0, of which waited for: 17 -> 0; matrix products, arithmetic and copies ran while one was open for 8% -> 0% of each run, Pallas kernels for 0% -> 0%
where the time goes in v1:
time: 102 us
  Pallas kernels  95.7 us (94%)
  local copies, waits for them, and re-layouts  5.2 us (5%)
    pallas_call x1, Pallas kernels, local(): pl.pallas_call(functools.partial(kernel, factor), out_shape=(shape((T, D)...  94.3 us
    unnamed x18, local copies, waits for them, and re-layouts  5.2 us

profile of v1, /device:TPU:1, one launch (start us, length us, event | category | flops | bytes accessed | tf_op | source)
XLA Modules:
  0.0 101.6 jit_solution(18173861043453277828)
XLA Ops:
  0.6 0.0 copy-start.5
  0.7 0.0 copy-start.6
  0.7 0.0 copy-start.7
  0.7 0.0 copy-start.8
  0.7 0.6 copy-done.5
  1.3 0.0 copy-done.6
  1.3 0.0 copy-done.7
  1.3 0.0 copy-done.8
  1.3 0.0 copy-start
  1.4 1.0 %copy-done = bf16[256,1024]{1,0:T(8,128)(2,1)S(1)} copy-done((bf16[256,1024]{1,0:T(8,128)(2,1)S(1)}, bf16[256,1024]{1,0:T(8,128)(2,1)}, u32[]{:S(2)}) %copy-start) | copy-done | bytes 524312
  2.4 0.0 copy-start.1
  2.4 0.9 copy-done.1
  3.3 0.0 copy-start.2
  3.3 0.9 copy-done.2
  4.2 0.0 copy-start.3
  4.2 0.9 copy-done.3
  5.2 0.0 copy-start.4
  5.2 0.7 copy-done.4
  5.9 94.3 %shard_map.160 = (bf16[256,256]{1,0:T(8,128)(2,1)S(1)}, bf16[256,256]{1,0:T(8,128)(2,1)S(1)}, f32[2048,128]{1,0:T(8,128)S(1)}, f32[1280,128]{1,0:T(8,128)S(1)}) custom-call(bf16[256,256]{1,0:T(8,128)(2,1)S(1)} %bitcast.14, bf16[256,256]{1,0:T(8,128)(2,1)S(1)} %bitcast.15, bf16[256,1024]{1,0:T(8,128)(2,1)S(1)} %copy-done, bf16[40,256]{1,0:T(8,128)(2,1)S(1)} %bitcast.16, ...), custom_call_target="tpu_custom_call" | custom-call | tf_op jit(solution)/shard_map/pallas_call | solution.py:671
  100.1 1.5 %shard_map.161 = (bf16[256,256]{1,0:T(8,128)(2,1)}, bf16[256,256]{1,0:T(8,128)(2,1)}, f32[256,1024]{1,0:T(8,128)}, f32[40,256]{1,0:T(8,128)}, f32[512,256]{1,0:T...) custom-call(f32[2048,128]{1,0:T(8,128)S(1)} %get-tuple-element.22.eres, ...), custom_call_target="tpu_custom_call" | custom-call | tf_op jit(solution)/shard_map/pallas_call | solution.py:691
Async XLA Ops:
  0.6 0.7 copy-start.5
  0.7 0.7 copy-start.6
  0.7 0.7 copy-start.7
  0.7 0.7 copy-start.8
  1.3 1.0 %copy-start = (bf16[256,1024]{1,0:T(8,128)(2,1)S(1)}, bf16[256,1024]{1,0:T(8,128)(2,1)}, u32[]{:S(2)}) copy-start(bf16[256,1024]{1,0:T(8,128)(2,1)} %refs_2_.1) | copy-start | bytes 1572868
  2.4 0.9 copy-start.1
  3.3 0.9 copy-start.2
  4.2 0.9 copy-start.3
  5.2 0.7 copy-start.4

commit v2 on v1

--- a/solution.py
+++ b/solution.py
@@ -307,6 +307,7 @@
 
 def kernel(factor, *refs):
     names_in = ["tok", "cot", "wi", "ws", "bias", "rate", "skip", "gain", "wo"]
+    names_in = [name + "_h" for name in names_in]
     names_out = ["lo", "gt", "eres", "lres"]
     n_io = len(names_in) + len(names_out)
     k = dict(zip(names_in + names_out, refs[:n_io]))
@@ -346,6 +347,12 @@
     ("es", pltpu.SemaphoreType.DMA((7, 9))), ("erv", pltpu.SemaphoreType.DMA((7, 9))),
     ("lsm", pltpu.SemaphoreType.DMA((7, 9))), ("lrv", pltpu.SemaphoreType.DMA((7, 9))),
 ]
+SCRATCH += [
+    ("tok", vm(T, D, dtype=BF16)), ("cot", vm(T, D, dtype=BF16)), ("wi", vm(D, 2 * E, dtype=BF16)),
+    ("ws", vm(2 * STATE + HEADS, D, dtype=BF16)), ("bias", vm(1, HEADS)), ("rate", vm(1, HEADS)),
+    ("skip", vm(1, HEADS)), ("gain", vm(1, E)), ("wo", vm(E, D, dtype=BF16)),
+    ("isem", pltpu.SemaphoreType.DMA((9,))),
+]
 RB = 32
 
 
@@ -356,13 +363,17 @@
     return lax.fori_loop(0, rows // RB, step, init)
 
 
-def body(factor, tok, cot, wi, ws, bias, rate, skip, gain, wo, lo, gt, eres, lres,
+def body(factor, tok_h, cot_h, wi_h, ws_h, bias_h, rate_h, skip_h, gain_h, wo_h, lo, gt, eres, lres,
          x, z, ub, stepe, bt, ct, s, ds, wsel, wpad, vecs, step, sig, cumr, cumc, cumrt, cumct,
          er, ec, wr, wc, dr, dc, dro, dco, finr, finc, finro, finco, wur, wuc, edr, edc, mr, mc, ls,
          yr, yc, car, cac, dn, dy, dyb, dzb, nb, qr, qc, dxb, dux, dbe, dce,
          own, got, into, send, ret, res, ebuf, ecb, exb, eyb, ezb, lbuf, lcb, lxb, lyb, lzb,
-         fsem, cs, cr, es, erv, lsm, lrv):
+         fsem, cs, cr, es, erv, lsm, lrv, tok, cot, wi, ws, bias, rate, skip, gain, wo, isem):
     pos = place()
+    given = (ws_h, ws), (bias_h, bias), (rate_h, rate), (skip_h, skip), (tok_h, tok), (wi_h, wi), (cot_h, cot), (wo_h, wo), (gain_h, gain)
+    fetch = [pltpu.make_async_copy(src, dst, isem.at[j]) for j, (src, dst) in enumerate(given)]
+    for copy in fetch:
+        copy.start()
     barrier = pltpu.get_barrier_semaphore()
     near = [at(pos, co=1 - pos["co"])] + peers(pos, "x") + peers(pos, "y") + peers(pos, "z")
     for to in near:
@@ -377,6 +388,8 @@
     early = Total(pos, ebuf, eres, ecb, exb, eyb, ezb, es, erv)
     late = Total(pos, lbuf, lres, lcb, lxb, lyb, lzb, lsm, lrv)
 
+    for copy in fetch[:6]:
+        copy.wait()
     r, c = grid2(2 * STATE + HEADS, 640)
     sel = ((c < 256) & (r == lo4(c))) | ((c >= 256) & (c < 512) & (r == 16 + lo4(c))) | ((c >= 512) & (r == c - 480))
     wsel[...] = mm(ws[...], ind(sel), 0, 0).astype(BF16)
@@ -484,6 +497,8 @@
         return carry
 
     lax.fori_loop(0, HEADS // 2, within, 0)
+    for copy in fetch[6:]:
+        copy.wait()
     dn[...] = mm(cot[...], wo[...], 1, 1)
     run_hops(fr, fc)
     fr.finish()
@@ -671,22 +686,27 @@
     lo, gt, eres, lres = pl.pallas_call(
         functools.partial(kernel, factor),
         out_shape=(shape((T, D), BF16), shape((T, D), BF16), shape((EARLY, 128), F32), shape((LATE, 128), F32)),
-        in_specs=[vmem] * 9,
+        in_specs=[pl.BlockSpec(memory_space=pltpu.HBM)] * 9,
         out_specs=(vmem,) * 4,
         scratch_shapes=[kind for _, kind in SCRATCH],
         compiler_params=pltpu.CompilerParams(
             collective_id=0, has_side_effects=True, vmem_limit_bytes=48 * 2**20
         ),
     )(
-        tokens_in.reshape(T, D),
-        out_cotangent.reshape(T, D),
-        w_inner,
-        w_ssm.T,
-        dt_bias.reshape(1, -1),
-        decay_rate.reshape(1, -1),
-        skip_gain.reshape(1, -1),
-        norm_gain.reshape(1, -1),
-        w_out,
+        *[
+            pltpu.with_memory_space_constraint(array, pltpu.HBM)
+            for array in (
+                tokens_in.reshape(T, D),
+                out_cotangent.reshape(T, D),
+                w_inner,
+                w_ssm.T,
+                dt_bias.reshape(1, -1),
+                decay_rate.reshape(1, -1),
+                skip_gain.reshape(1, -1),
+                norm_gain.reshape(1, -1),
+                w_out,
+            )
+        ]
     )
     out = pl.pallas_call(
         unpack,

time: 102 us -> 97.7 us (0.958)
  local copies, waits for them, and re-layouts: 5.2 us -> 0 us
  Pallas kernels: 95.7 us -> 96.9 us
    unnamed x18 -> x0, local copies, waits for them, and re-layouts: 5.2 us -> none
    pallas_call x1, Pallas kernels: 94.3 us -> 95.4 us  [local(): pl.pallas_call(functools.partial(kernel, factor), out_shape=(shape((T, D)...]
where the time goes in v2:
time: 97.7 us; the launch traced here: 97.5 us
  Pallas kernels  96.9 us (99%)
    pallas_call x1, Pallas kernels, local(): pl.pallas_call(functools.partial(kernel, factor), out_shape=(shape((T, D)...  95.4 us

profile of v2, /device:TPU:1, one launch (start us, length us, event | category | flops | bytes accessed | tf_op | source)
XLA Modules:
  0.0 97.5 jit_solution(796459947070756832)
XLA Ops:
  0.6 95.4 %shard_map.160 = (bf16[256,256]{1,0:T(8,128)(2,1)S(1)}, bf16[256,256]{1,0:T(8,128)(2,1)S(1)}, f32[2048,128]{1,0:T(8,128)S(1)}, f32[1280,128]{1,0:T(8,128)S(1)}) custom-call(bf16[256,256]{1,0:T(8,128)(2,1)} %bitcast.14, bf16[256,256]{1,0:T(8,128)(2,1)} %bitcast.15, bf16[256,1024]{1,0:T(8,128)(2,1)} %refs_2_.1, bf16[40,256]{1,0:T(8,128)(2,1)} %bitcast.16, ...), custom_call_target="tpu_custom_call" | custom-call | tf_op jit(solution)/shard_map/pallas_call | solution.py:686
  96.1 1.5 %shard_map.161 = (bf16[256,256]{1,0:T(8,128)(2,1)}, bf16[256,256]{1,0:T(8,128)(2,1)}, f32[256,1024]{1,0:T(8,128)}, f32[40,256]{1,0:T(8,128)}, f32[512,256]{1,0:T...) custom-call(f32[2048,128]{1,0:T(8,128)S(1)} %get-tuple-element.22.eres, ...), custom_call_target="tpu_custom_call" | custom-call | tf_op jit(solution)/shard_map/pallas_call | solution.py:711

commit v3 on v2

--- a/solution.py
+++ b/solution.py
@@ -17,8 +17,8 @@
 T = SIDE * SIDE
 E = HEADS * HDIM
 D = 256
-CH = 4
-CR = 128 // CH
+TILES = 8
+SHARE = T // TILES
 NEG = -1e30
 EARLY = 2048
 LATE = 1280
@@ -129,103 +129,57 @@
     )
 
 
-class Chain:
-    def __init__(self, pos, axis, back, own, got, into, send, ret, res, dec, deco, ssem, rsem, slot):
-        self.bit, step = ("co", "z") if axis == "r" else ("xh", "y")
-        b, q = pos[self.bit], pos[step]
-        self.b = b
-        self.first = (b == 1) if back else (b == 0)
-        self.r = (3 - q) if back else q
-        self.nxt = at(pos, **{step: lax.rem(q + (3 if back else 1), 4)})
-        self.partner = at(pos, **{self.bit: 1 - b})
-        self.own, self.got, self.into, self.send, self.ret, self.res = own, got, into, send, ret, res
-        self.dec, self.deco = dec, deco
+class Scan:
+    def __init__(self, pos, axis, back, own, got, out, res, dec, ssem, rsem, slot):
+        self.me = lax.axis_index("col" if axis == "r" else "row")
+        self.pos, self.axis, self.back = pos, axis, back
+        self.own, self.got, self.out, self.res, self.dec = own, got, out, res, dec
         self.ssem, self.rsem, self.slot = ssem, rsem, slot
 
-    def half(self, mine, c):
-        start = (self.b if mine else 1 - self.b) * 128 + c * CR
-        return pl.ds(pl.multiple_of(start, CR), CR)
-
-    def sems(self, stage, c):
-        return self.ssem.at[self.slot, stage, c], self.rsem.at[self.slot, stage, c]
-
-    def c_exch(self, c):
-        return remote(self.own.at[self.half(False, c)], self.got.at[pl.ds(c * CR, CR)], *self.sems(0, c), self.partner)
-
-    def c_hop(self, c):
-        return remote(self.send.at[pl.ds(c * CR, CR)], self.into.at[pl.ds(c * CR, CR)], *self.sems(1, c), self.nxt)
-
-    def c_ret(self, c):
-        return remote(self.ret.at[pl.ds(c * CR, CR)], self.res.at[self.half(True, c)], *self.sems(2, c), self.partner)
+    def peer(self, d):
+        k = lax.rem(self.me + d, TILES)
+        if self.axis == "r":
+            return k, (lax.axis_index("row"), k, self.pos["xl"])
+        return k, (k, lax.axis_index("col"), self.pos["xl"])
+
+    def lines(self, k):
+        return pl.ds(pl.multiple_of(k * SHARE, SHARE), SHARE)
+
+    def copies(self, stage):
+        out = []
+        for d in (4, 3, 5, 2, 6, 1, 7):
+            k, to = self.peer(d)
+            sems = self.ssem.at[self.slot, stage, d], self.rsem.at[self.slot, stage, d]
+            if stage == 0:
+                out.append(remote(self.own.at[self.lines(k)], self.got.at[self.me], *sems, to))
+            else:
+                out.append(remote(self.out.at[k], self.res.at[self.lines(self.me)], *sems, to))
+        return out
 
     def start(self):
-        @pl.when(self.r == 0)
-        def _():
-            self.into[...] = jnp.zeros((128, E), F32)
-
-        for c in range(CH):
-            self.c_exch(c).start()
-
-    def pair(self, c):
-        sl = pl.ds(c * CR, CR)
-        self.c_exch(c).wait_recv()
-        got, own = self.got[sl], self.own[self.half(True, c)]
-        d_own, d_oth = self.dec[self.half(True, c)], self.deco[sl]
-        lead = jnp.where(self.first, own, got)
-        tail = jnp.where(self.first, got, own)
-        d_tail = jnp.where(self.first, d_oth, d_own)
-        self.send[sl] = tail + d_tail * lead
-
-        @pl.when(self.r == 0)
-        def _():
-            self.c_hop(c).start()
-
-    def hop(self, c):
-        sl = pl.ds(c * CR, CR)
-
-        @pl.when(self.r > 0)
-        def _():
-            self.c_hop(c).wait_recv()
-
-        enter = self.into[sl]
-        d_own, d_oth = self.dec[self.half(True, c)], self.deco[sl]
-
-        @pl.when((self.r > 0) & (self.r < 3))
-        def _():
-            self.send[sl] = self.send[sl] + d_own * d_oth * enter
-            self.c_hop(c).start()
-
-        lead = jnp.where(self.first, self.own[self.half(True, c)], self.got[sl])
-        d_lead = jnp.where(self.first, d_own, d_oth)
-        after = d_lead * enter + lead
-        self.ret[sl] = jnp.where(self.first, after, enter)
-        self.c_ret(c).start()
-        self.res[self.half(True, c)] = jnp.where(self.first, enter, after)
+        for copy in self.copies(0):
+            copy.start()
+        self.got[self.me] = self.own[self.lines(self.me)]
+
+    def turn(self):
+        for copy in self.copies(0):
+            copy.wait_recv()
+        state = jnp.zeros((SHARE, E), F32)
+        for j in range(TILES - 1, -1, -1) if self.back else range(TILES):
+            self.out[j] = state
+            state = self.dec[j * SHARE : (j + 1) * SHARE] * state + self.got[j]
+        for copy in self.copies(1):
+            copy.start()
+        self.res[self.lines(self.me)] = self.out[self.me]
 
     def finish(self):
-        for c in range(CH):
-            self.c_ret(c).wait_recv()
+        for copy in self.copies(1):
+            copy.wait_recv()
 
     def drain(self):
-        for c in range(CH):
-            self.c_exch(c).wait_send()
-            self.c_ret(c).wait_send()
-
-            @pl.when(self.r < 3)
-            def _():
-                self.c_hop(c).wait_send()
-
-
-def run_hops(a, c):
-    @pl.when(a.r <= c.r)
-    def _():
-        for who, at_chunk in ((a, 0), (a, 1), (c, 0), (a, 2), (c, 1), (a, 3), (c, 2), (c, 3)):
-            who.hop(at_chunk)
-
-    @pl.when(a.r > c.r)
-    def _():
-        for who, at_chunk in ((c, 0), (c, 1), (a, 0), (c, 2), (a, 1), (c, 3), (a, 2), (a, 3)):
-            who.hop(at_chunk)
+        for stage in (0, 1):
+            for copy in self.copies(stage):
+                copy.wait_send()
 
 
 class Total:
@@ -327,8 +281,8 @@
     ("step", vm(T, 128)), ("sig", vm(T, 128)),
     ("cumr", vm(T, 128)), ("cumc", vm(T, 128)), ("cumrt", vm(128, T)), ("cumct", vm(128, T)),
     ("er", vm(*BIG)), ("ec", vm(*BIG)), ("wr", vm(*BIG)), ("wc", vm(*BIG)), ("dr", vm(*BIG)), ("dc", vm(*BIG)),
-    ("dro", vm(128, E)), ("dco", vm(128, E)),
-    ("finr", vm(SIDE, 128)), ("finc", vm(SIDE, 128)), ("finro", vm(SIDE, 128)), ("finco", vm(SIDE, 128)),
+    ("dxr", vm(*BIG)), ("dxc", vm(*BIG)),
+    ("finr", vm(SIDE, 128)), ("finc", vm(SIDE, 128)), ("allr", vm(128, 128)), ("allc", vm(128, 128)),
     ("wur", vm(2, *BIG, dtype=BF16)), ("wuc", vm(2, *BIG, dtype=BF16)),
     ("edr", vm(2, *BIG, dtype=BF16)), ("edc", vm(2, *BIG, dtype=BF16)),
     ("mr", vm(2, HEADS, T, T, dtype=BF16)), ("mc", vm(2, HEADS, T, T, dtype=BF16)), ("ls", vm(HEADS, T, T)),
@@ -336,14 +290,14 @@
     ("dy", vm(*BIG)), ("dyb", vm(2, *BIG, dtype=BF16)), ("dzb", vm(*BIG, dtype=BF16)), ("nb", vm(*BIG, dtype=BF16)),
     ("qr", vm(*BIG)), ("qc", vm(*BIG)), ("dxb", vm(*BIG, dtype=BF16)), ("dux", vm(*BIG)),
     ("dbe", vm(T, T)), ("dce", vm(T, T)),
-    ("own", pltpu.VMEM((4, T, E), F32)), ("got", pltpu.VMEM((4, 128, E), F32)), ("into", pltpu.VMEM((4, 128, E), F32)),
-    ("send", pltpu.VMEM((4, 128, E), F32)), ("ret", pltpu.VMEM((4, 128, E), F32)), ("res", pltpu.VMEM((4, T, E), F32)),
+    ("own", pltpu.VMEM((4, T, E), F32)), ("got", pltpu.VMEM((4, TILES, SHARE, E), F32)),
+    ("out", pltpu.VMEM((4, TILES, SHARE, E), F32)), ("res", pltpu.VMEM((4, T, E), F32)),
     ("ebuf", vm(EARLY, 128)), ("ecb", vm(EARLY // 2, 128)), ("exb", vm(3, EARLY // 8, 128)),
     ("eyb", vm(3, EARLY // 32, 128)), ("ezb", vm(3, EARLY // 32, 128)),
     ("lbuf", vm(LATE, 128)), ("lcb", vm(LATE // 2, 128)), ("lxb", vm(3, LATE // 8, 128)),
     ("lyb", vm(3, LATE // 32, 128)), ("lzb", vm(3, LATE // 32, 128)),
-    ("fsem", pltpu.SemaphoreType.DMA((2, 2))),
-    ("cs", pltpu.SemaphoreType.DMA((4, 3, CH))), ("cr", pltpu.SemaphoreType.DMA((4, 3, CH))),
+    ("fsem", pltpu.SemaphoreType.DMA((2, 2, TILES))),
+    ("cs", pltpu.SemaphoreType.DMA((4, 2, TILES))), ("cr", pltpu.SemaphoreType.DMA((4, 2, TILES))),
     ("es", pltpu.SemaphoreType.DMA((7, 9))), ("erv", pltpu.SemaphoreType.DMA((7, 9))),
     ("lsm", pltpu.SemaphoreType.DMA((7, 9))), ("lrv", pltpu.SemaphoreType.DMA((7, 9))),
 ]
@@ -365,9 +319,9 @@
 
 def body(factor, tok_h, cot_h, wi_h, ws_h, bias_h, rate_h, skip_h, gain_h, wo_h, lo, gt, eres, lres,
          x, z, ub, stepe, bt, ct, s, ds, wsel, wpad, vecs, step, sig, cumr, cumc, cumrt, cumct,
-         er, ec, wr, wc, dr, dc, dro, dco, finr, finc, finro, finco, wur, wuc, edr, edc, mr, mc, ls,
+         er, ec, wr, wc, dr, dc, dxr, dxc, finr, finc, allr, allc, wur, wuc, edr, edc, mr, mc, ls,
          yr, yc, car, cac, dn, dy, dyb, dzb, nb, qr, qc, dxb, dux, dbe, dce,
-         own, got, into, send, ret, res, ebuf, ecb, exb, eyb, ezb, lbuf, lcb, lxb, lyb, lzb,
+         own, got, out, res, ebuf, ecb, exb, eyb, ezb, lbuf, lcb, lxb, lyb, lzb,
          fsem, cs, cr, es, erv, lsm, lrv, tok, cot, wi, ws, bias, rate, skip, gain, wo, isem):
     pos = place()
     given = (ws_h, ws), (bias_h, bias), (rate_h, rate), (skip_h, skip), (tok_h, tok), (wi_h, wi), (cot_h, cot), (wo_h, wo), (gain_h, gain)
@@ -375,16 +329,16 @@
     for copy in fetch:
         copy.start()
     barrier = pltpu.get_barrier_semaphore()
-    near = [at(pos, co=1 - pos["co"])] + peers(pos, "x") + peers(pos, "y") + peers(pos, "z")
+
+    def scan(slot, axis, back):
+        return Scan(pos, axis, back, own.at[slot], got.at[slot], out.at[slot], res.at[slot], (dxr, dxc)[slot % 2],
+                    cs, cr, slot)
+
+    fr, fc, gr_, gc_ = scan(0, "r", False), scan(1, "c", False), scan(2, "r", True), scan(3, "c", True)
+    near = [who.peer(d)[1] for who in (fr, fc) for d in range(1, TILES)]
+    near += [at(pos, xl=1 - pos["xl"]), at(pos, xl=1 - pos["xl"], xh=1 - pos["xh"])]
     for to in near:
         pl.semaphore_signal(barrier, inc=1, device_id=to, device_id_type=MESH)
-
-    def chain(slot, axis, back):
-        a = slot % 2
-        return Chain(pos, axis, back, own.at[slot], got.at[slot], into.at[slot], send.at[slot], ret.at[slot],
-                     res.at[slot], (dr, dc)[a], (dro, dco)[a], cs, cr, slot)
-
-    fr, fc, gr_, gc_ = chain(0, "r", False), chain(1, "c", False), chain(2, "r", True), chain(3, "c", True)
     early = Total(pos, ebuf, eres, ecb, exb, eyb, ezb, es, erv)
     late = Total(pos, lbuf, lres, lcb, lxb, lyb, lzb, lsm, lrv)
 
@@ -433,12 +387,15 @@
     own[1] = mm3(only(line_c, bt), both(wuc), 0, 0)
     own[0] = mm3(only(line_r, bt), both(wur), 0, 0)
     pl.semaphore_wait(barrier, len(near))
-    f_r = remote(finr, finro, fsem.at[0, 0], fsem.at[0, 1], fr.partner)
-    f_c = remote(finc, finco, fsem.at[1, 0], fsem.at[1, 1], fc.partner)
-    f_r.start()
-    f_c.start()
+    ends = []
+    for a_, (who, mine, all_) in enumerate(((fc, finc, allc), (fr, finr, allr))):
+        place_ = pl.ds(pl.multiple_of(who.me * SIDE, SIDE), SIDE)
+        all_[place_] = mine[...]
+        for d in range(1, TILES):
+            ends.append(remote(mine, all_.at[place_], fsem.at[a_, 0, d], fsem.at[a_, 1, d], who.peer(d)[1]))
+            ends[-1].start()
+    fc.start()
     fr.start()
-    fc.start()
 
     def lines(rows, first, ends):
         k, l = grid2(rows, SIDE)
@@ -446,10 +403,6 @@
 
     dr[...] = lines(T, 0, finr[...])
     dc[...] = lines(T, 0, finc[...])
-    f_r.wait_recv()
-    dro[...] = lines(128, pos["co"] * 8, finro[...])
-    for q in range(CH):
-        fr.pair(q)
 
     z[...] = mm(tok[...], wi[:, E : 2 * E])
     keep(ct, (), mm(tok[...], wsel[:, 256:512]))
@@ -475,10 +428,6 @@
         return carry
 
     loop(T, masks)
-    f_c.wait_recv()
-    dco[...] = lines(128, pos["xh"] * 8, finco[...])
-    for q in range(CH):
-        fc.pair(q)
     low = lax.broadcasted_iota(jnp.int32, (T, 128), 1) < HDIM
 
     def heads(m, hp, pair, dim):
@@ -496,11 +445,19 @@
         yc[:, sl] = heads(mc, hp, u_, 1)
         return carry
 
-    lax.fori_loop(0, HEADS // 2, within, 0)
     for copy in fetch[6:]:
         copy.wait()
+
+    for copy in ends:
+        copy.wait_recv()
+    k, l = grid2(T, 128)
+    line = lax.shift_right_logical(k, 5) * SIDE + jnp.bitwise_and(hi4(k), 1)
+    for who, all_ in ((fr, allr), (fc, allc)):
+        who.dec[...] = spread(pick(ind(l == line + 2 * who.me), all_[...], 2), hx)
+    fr.turn()
+    fc.turn()
+    lax.fori_loop(0, HEADS // 2, within, 0)
     dn[...] = mm(cot[...], wo[...], 1, 1)
-    run_hops(fr, fc)
     fr.finish()
     car[...] = mm3(only(line_r, ct), split(res[0], 2))
     fc.finish()
@@ -549,10 +506,6 @@
     for j in range(2):
         ebuf[1024 + j * 512 : 1024 + (j + 1) * 512] = lg[:, j * 128 : (j + 1) * 128]
     early.start(0)
-    for q in range(CH):
-        gr_.pair(q)
-    early.step(0)
-
     def within_back(hp, carry):
         sl = pl.ds(pl.multiple_of(hp * 128, 128), 128)
         d_ = (dyb[0, :, sl], dyb[1, :, sl])
@@ -560,10 +513,6 @@
         yc[:, sl] = heads(mc, hp, d_, 0)
         return carry
 
-    lax.fori_loop(0, HEADS // 2, within_back, 0)
-    for q in range(CH):
-        gc_.pair(q)
-    ds[...] = jnp.zeros((T, T), F32)
 
     def scores_back(hp, carry):
         sl = pl.ds(pl.multiple_of(hp * 128, 128), 128)
@@ -577,6 +526,11 @@
         ds[...] = total
         return carry
 
+    lax.fori_loop(0, HEADS // 2, within_back, 0)
+    gr_.turn()
+    gc_.turn()
+    early.step(0)
+    ds[...] = jnp.zeros((T, T), F32)
     lax.fori_loop(0, HEADS // 2, scores_back, 0)
     head = u < STATE
     d_s = split(ds[...], 2)
@@ -587,7 +541,6 @@
     )
     dbe[...] = jnp.where(head, mm3(d_s, both(ct), 0, 0), 0.0)
     lo[...] = mm(nb[...], wo[...]).astype(BF16)
-    run_hops(gr_, gc_)
     early.step(1)
     gr_.finish()
     g_r = split(res[2], 2)
@@ -656,8 +609,8 @@
     late.step(3)
     for who in (fr, fc, gr_, gc_):
         who.drain()
-    f_r.wait_send()
-    f_c.wait_send()
+    for copy in ends:
+        copy.wait_send()
     late.step(4)
     late.step(5)
     late.step(6)

time: 97.7 us -> 84 us (0.86)
  Pallas kernels: 96.9 us -> 83.2 us
    pallas_call x1, Pallas kernels: 95.4 us -> 81.8 us  [local(): pl.pallas_call(functools.partial(kernel, factor), out_shape=(shape((T, D)...]
where the time goes in v3:
time: 84 us; the launch traced here: 83.9 us
  Pallas kernels  83.2 us (99%)
    pallas_call x1, Pallas kernels, local(): pl.pallas_call(functools.partial(kernel, factor), out_shape=(shape((T, D)...  81.8 us

profile of v3, /device:TPU:1, one launch (start us, length us, event | category | flops | bytes accessed | tf_op | source)
XLA Modules:
  0.0 83.9 jit_solution(8788262894202624151)
XLA Ops:
  0.6 81.8 %shard_map.160 = (bf16[256,256]{1,0:T(8,128)(2,1)S(1)}, bf16[256,256]{1,0:T(8,128)(2,1)S(1)}, f32[2048,128]{1,0:T(8,128)S(1)}, f32[1280,128]{1,0:T(8,128)S(1)}) custom-call(bf16[256,256]{1,0:T(8,128)(2,1)} %bitcast.14, bf16[256,256]{1,0:T(8,128)(2,1)} %bitcast.15, bf16[256,1024]{1,0:T(8,128)(2,1)} %refs_2_.1, bf16[40,256]{1,0:T(8,128)(2,1)} %bitcast.16, ...), custom_call_target="tpu_custom_call" | custom-call | tf_op jit(solution)/shard_map/pallas_call | solution.py:639
  82.4 1.5 %shard_map.161 = (bf16[256,256]{1,0:T(8,128)(2,1)}, bf16[256,256]{1,0:T(8,128)(2,1)}, f32[256,1024]{1,0:T(8,128)}, f32[40,256]{1,0:T(8,128)}, f32[512,256]{1,0:T...) custom-call(f32[2048,128]{1,0:T(8,128)S(1)} %get-tuple-element.22.eres, ...), custom_call_target="tpu_custom_call" | custom-call | tf_op jit(solution)/shard_map/pallas_call | solution.py:664

commit v4 on v3

--- a/solution.py
+++ b/solution.py
@@ -19,9 +19,13 @@
 D = 256
 TILES = 8
 SHARE = T // TILES
+PARTS = SHARE // STATE
 NEG = -1e30
 EARLY = 2048
 LATE = 1280
+LROW = (0, 256, 640, 896)
+SROW = (512, 1152)
+VROW = 512 + 64
 
 
 def mm(a, b, ca=1, cb=0):
@@ -142,44 +146,46 @@
             return k, (lax.axis_index("row"), k, self.pos["xl"])
         return k, (k, lax.axis_index("col"), self.pos["xl"])
 
-    def lines(self, k):
-        return pl.ds(pl.multiple_of(k * SHARE, SHARE), SHARE)
-
-    def copies(self, stage):
-        out = []
+    def lines(self, k, part):
+        return pl.ds(pl.multiple_of(k * SHARE + part * STATE, STATE), STATE)
+
+    def copies(self, stage, part):
+        out, piece = [], pl.ds(part * STATE, STATE)
         for d in (4, 3, 5, 2, 6, 1, 7):
             k, to = self.peer(d)
-            sems = self.ssem.at[self.slot, stage, d], self.rsem.at[self.slot, stage, d]
+            sems = self.ssem.at[self.slot, stage, part, d], self.rsem.at[self.slot, stage, part, d]
             if stage == 0:
-                out.append(remote(self.own.at[self.lines(k)], self.got.at[self.me], *sems, to))
+                out.append(remote(self.own.at[self.lines(k, part)], self.got.at[self.me, piece], *sems, to))
             else:
-                out.append(remote(self.out.at[k], self.res.at[self.lines(self.me)], *sems, to))
+                out.append(remote(self.out.at[k, piece], self.res.at[self.lines(self.me, part)], *sems, to))
         return out
 
-    def start(self):
-        for copy in self.copies(0):
+    def start(self, part):
+        for copy in self.copies(0, part):
             copy.start()
-        self.got[self.me] = self.own[self.lines(self.me)]
-
-    def turn(self):
-        for copy in self.copies(0):
+        self.got[self.me, pl.ds(part * STATE, STATE)] = self.own[self.lines(self.me, part)]
+
+    def turn(self, part):
+        for copy in self.copies(0, part):
             copy.wait_recv()
-        state = jnp.zeros((SHARE, E), F32)
+        state, piece = jnp.zeros((STATE, E), F32), pl.ds(part * STATE, STATE)
         for j in range(TILES - 1, -1, -1) if self.back else range(TILES):
-            self.out[j] = state
-            state = self.dec[j * SHARE : (j + 1) * SHARE] * state + self.got[j]
-        for copy in self.copies(1):
+            self.out[j, piece] = state
+            state = self.dec[pl.ds(j * SHARE + part * STATE, STATE)] * state + self.got[j, piece]
+        for copy in self.copies(1, part):
             copy.start()
-        self.res[self.lines(self.me)] = self.out[self.me]
+        self.res[self.lines(self.me, part)] = self.out[self.me, piece]
 
     def finish(self):
-        for copy in self.copies(1):
-            copy.wait_recv()
+        for part in range(PARTS):
+            for copy in self.copies(1, part):
+                copy.wait_recv()
 
     def drain(self):
         for stage in (0, 1):
-            for copy in self.copies(stage):
-                copy.wait_send()
+            for part in range(PARTS):
+                for copy in self.copies(stage, part):
+                    copy.wait_send()
 
 
 class Total:
@@ -297,7 +303,7 @@
     ("lbuf", vm(LATE, 128)), ("lcb", vm(LATE // 2, 128)), ("lxb", vm(3, LATE // 8, 128)),
     ("lyb", vm(3, LATE // 32, 128)), ("lzb", vm(3, LATE // 32, 128)),
     ("fsem", pltpu.SemaphoreType.DMA((2, 2, TILES))),
-    ("cs", pltpu.SemaphoreType.DMA((4, 2, TILES))), ("cr", pltpu.SemaphoreType.DMA((4, 2, TILES))),
+    ("cs", pltpu.SemaphoreType.DMA((4, 2, PARTS, TILES))), ("cr", pltpu.SemaphoreType.DMA((4, 2, PARTS, TILES))),
     ("es", pltpu.SemaphoreType.DMA((7, 9))), ("erv", pltpu.SemaphoreType.DMA((7, 9))),
     ("lsm", pltpu.SemaphoreType.DMA((7, 9))), ("lrv", pltpu.SemaphoreType.DMA((7, 9))),
 ]
@@ -361,8 +367,6 @@
     a = -stp * vecs[1:2, :]
     t, u = grid2(T, T)
     same_r, same_c = hi4(t) == hi4(u), lo4(t) == lo4(u)
-    cumr[...] = pick(ind(same_r & (u <= t)), a)
-    cumc[...] = pick(ind(same_c & (u <= t)), a)
     aft_r = pick(ind(same_r & (u > t)), a)
     aft_c = pick(ind(same_c & (u > t)), a)
     r, c = grid2(SIDE, T)
@@ -394,8 +398,12 @@
         for d in range(1, TILES):
             ends.append(remote(mine, all_.at[place_], fsem.at[a_, 0, d], fsem.at[a_, 1, d], who.peer(d)[1]))
             ends[-1].start()
-    fc.start()
-    fr.start()
+    for part in range(PARTS):
+        fc.start(part)
+        fr.start(part)
+
+    cumr[...] = pick(ind(same_r & (u <= t)), a)
+    cumc[...] = pick(ind(same_c & (u <= t)), a)
 
     def lines(rows, first, ends):
         k, l = grid2(rows, SIDE)
@@ -454,8 +462,9 @@
     line = lax.shift_right_logical(k, 5) * SIDE + jnp.bitwise_and(hi4(k), 1)
     for who, all_ in ((fr, allr), (fc, allc)):
         who.dec[...] = spread(pick(ind(l == line + 2 * who.me), all_[...], 2), hx)
-    fr.turn()
-    fc.turn()
+    for part in range(PARTS):
+        fr.turn(part)
+        fc.turn(part)
     lax.fori_loop(0, HEADS // 2, within, 0)
     dn[...] = mm(cot[...], wo[...], 1, 1)
     fr.finish()
@@ -495,9 +504,11 @@
     nil = jnp.zeros((8, E), F32)
     sum_gain, sum_skip = loop(T, middle, (nil, nil))
     own[3] = mm3(only(line_c, ct), both(edc), 0, 0)
-    gc_.start()
+    for part in range(PARTS):
+        gc_.start(part)
     own[2] = mm3(only(line_r, ct), both(edr), 0, 0)
-    gr_.start()
+    for part in range(PARTS):
+        gr_.start(part)
 
     lg = mm(tok[...], dzb[...], 0, 0) * factor
     for j in range(4):
@@ -527,9 +538,9 @@
         return carry
 
     lax.fori_loop(0, HEADS // 2, within_back, 0)
-    gr_.turn()
-    gc_.turn()
-    early.step(0)
+    for part in range(PARTS):
+        gr_.turn(part)
+        gc_.turn(part)
     ds[...] = jnp.zeros((T, T), F32)
     lax.fori_loop(0, HEADS // 2, scores_back, 0)
     head = u < STATE
@@ -541,13 +552,12 @@
     )
     dbe[...] = jnp.where(head, mm3(d_s, both(ct), 0, 0), 0.0)
     lo[...] = mm(nb[...], wo[...]).astype(BF16)
-    early.step(1)
     gr_.finish()
     g_r = split(res[2], 2)
     car[...] = mm3(only(line_r, bt), g_r)
     dbe[...] = dbe[...] + jnp.where(line_r, mm3(both(wur), g_r, 1, 1), 0.0)
-    early.step(2)
     gc_.finish()
+    early.step(0)
     g_c = split(res[3], 2)
     cac[...] = mm3(only(line_c, bt), g_c)
     dbe[...] = dbe[...] + jnp.where(line_c, mm3(both(wuc), g_c, 1, 1), 0.0)
@@ -569,7 +579,7 @@
     loop(T, last)
     lg = mm(tok[...], dxb[...], 0, 0) * factor
     for j in range(4):
-        lbuf[j * 256 : (j + 1) * 256] = lg[:, j * 128 : (j + 1) * 128]
+        lbuf[LROW[j] : LROW[j] + 256] = lg[:, j * 128 : (j + 1) * 128]
     d_a = (
         pick(ind(same_r & (u >= t)), head_sum(qr[...]))
         + pick(ind(same_c & (u >= t)), head_sum(qc[...]))
@@ -587,31 +597,34 @@
     d_ssm = d_ssm.astype(BF16)
     lg = mm(d_ssm, tok[...], 0, 0) * factor
     for j in range(2):
-        lbuf[1024 + j * 128 : 1152 + j * 128] = lg[:, j * 128 : (j + 1) * 128]
+        lbuf[SROW[j] : SROW[j] + 128] = lg[:, j * 128 : (j + 1) * 128]
     total_of = lambda v: jnp.sum(v, axis=0, keepdims=True)
     sum_gain = total_of(sum_gain) * factor
     for j in range(4):
-        lbuf[1088 + j : 1089 + j] = sum_gain[:, j * 128 : (j + 1) * 128]
-    lbuf[1092:1093] = total_of(d_raw) * factor
-    lbuf[1093:1094] = -total_of(step[...] * d_a) * factor
-    lbuf[1094:1095] = total_of(head_sum(sum_skip)) * factor
+        lbuf[VROW + j : VROW + j + 1] = sum_gain[:, j * 128 : (j + 1) * 128]
+    lbuf[VROW + 4 : VROW + 5] = total_of(d_raw) * factor
+    lbuf[VROW + 5 : VROW + 6] = -total_of(step[...] * d_a) * factor
+    lbuf[VROW + 6 : VROW + 7] = total_of(head_sum(sum_skip)) * factor
     late.start(0)
-    early.step(3)
+    early.step(1)
+    back = mm(dxb[...], wi[:, 0:E], 1, 1)
     late.step(0)
-    back = mm(dxb[...], wi[:, 0:E], 1, 1) + mm(dzb[...], wi[:, E : 2 * E], 1, 1)
+    back = back + mm(dzb[...], wi[:, E : 2 * E], 1, 1)
     back = back + mm(d_ssm, wpad[...], 1, 1)
     gt[...] = back.astype(BF16)
+    early.step(2)
+    late.step(1)
+    early.step(3)
+    late.step(2)
     early.step(4)
-    late.step(1)
+    late.step(3)
     early.step(5)
-    late.step(2)
-    early.step(6)
-    late.step(3)
     for who in (fr, fc, gr_, gc_):
         who.drain()
     for copy in ends:
         copy.wait_send()
     late.step(4)
+    early.finish(6)
     late.step(5)
     late.step(6)
 
@@ -620,15 +633,15 @@
     lo[...] = lo_in[...]
     gt[...] = gt_in[...]
     for j in range(4):
-        gi[:, j * 128 : (j + 1) * 128] = lres[j * 256 : (j + 1) * 256]
+        gi[:, j * 128 : (j + 1) * 128] = lres[LROW[j] : LROW[j] + 256]
         gi[:, E + j * 128 : E + (j + 1) * 128] = eres[j * 256 : (j + 1) * 256]
-        gg[:, j * 128 : (j + 1) * 128] = lres[1088 + j : 1089 + j]
+        gg[:, j * 128 : (j + 1) * 128] = lres[VROW + j : VROW + j + 1]
     for j in range(2):
         go[:, j * 128 : (j + 1) * 128] = eres[1024 + j * 512 : 1024 + (j + 1) * 512]
-        gs[:, j * 128 : (j + 1) * 128] = lres[1024 + j * 128 : 1064 + j * 128]
-    gb[...] = lres[1092:1093, 0:HEADS]
-    gr[...] = lres[1093:1094, 0:HEADS]
-    gk[...] = lres[1094:1095, 0:HEADS]
+        gs[:, j * 128 : (j + 1) * 128] = lres[SROW[j] : SROW[j] + 40]
+    gb[...] = lres[VROW + 4 : VROW + 5, 0:HEADS]
+    gr[...] = lres[VROW + 5 : VROW + 6, 0:HEADS]
+    gk[...] = lres[VROW + 6 : VROW + 7, 0:HEADS]
 
 
 def local(tokens_in, out_cotangent, w_inner, w_ssm, dt_bias, decay_rate, skip_gain, norm_gain, w_out):

time: 84 us -> 76.9 us (0.915)
  Pallas kernels: 83.2 us -> 76.1 us
    pallas_call x1, Pallas kernels: 81.8 us -> 74.7 us  [local(): pl.pallas_call(functools.partial(kernel, factor), out_shape=(shape((T, D)...]
where the time goes in v4:
time: 76.9 us; the launch traced here: 76.8 us
  Pallas kernels  76.1 us (99%)
    pallas_call x1, Pallas kernels, local(): pl.pallas_call(functools.partial(kernel, factor), out_shape=(shape((T, D)...  74.7 us

profile of v4, /device:TPU:1, one launch (start us, length us, event | category | flops | bytes accessed | tf_op | source)
XLA Modules:
  0.0 76.8 jit_solution(1548389941243077784)
XLA Ops:
  0.6 74.7 %shard_map.160 = (bf16[256,256]{1,0:T(8,128)(2,1)S(1)}, bf16[256,256]{1,0:T(8,128)(2,1)S(1)}, f32[2048,128]{1,0:T(8,128)S(1)}, f32[1280,128]{1,0:T(8,128)S(1)}) custom-call(bf16[256,256]{1,0:T(8,128)(2,1)} %bitcast.14, bf16[256,256]{1,0:T(8,128)(2,1)} %bitcast.15, bf16[256,1024]{1,0:T(8,128)(2,1)} %refs_2_.1, bf16[40,256]{1,0:T(8,128)(2,1)} %bitcast.16, ...), custom_call_target="tpu_custom_call" | custom-call | tf_op jit(solution)/shard_map/pallas_call | solution.py:652
  75.3 1.5 %shard_map.161 = (bf16[256,256]{1,0:T(8,128)(2,1)}, bf16[256,256]{1,0:T(8,128)(2,1)}, f32[256,1024]{1,0:T(8,128)}, f32[40,256]{1,0:T(8,128)}, f32[512,256]{1,0:T...) custom-call(f32[2048,128]{1,0:T(8,128)S(1)} %get-tuple-element.22.eres, ...), custom_call_target="tpu_custom_call" | custom-call | tf_op jit(solution)/shard_map/pallas_call | solution.py:677

commit v5 on v4

--- a/solution.py
+++ b/solution.py
@@ -20,6 +20,7 @@
 TILES = 8
 SHARE = T // TILES
 PARTS = SHARE // STATE
+ORDER = (4, 3, 5, 2, 6, 1, 7)
 NEG = -1e30
 EARLY = 2048
 LATE = 1280
@@ -137,6 +138,7 @@
     def __init__(self, pos, axis, back, own, got, out, res, dec, ssem, rsem, slot):
         self.me = lax.axis_index("col" if axis == "r" else "row")
         self.pos, self.axis, self.back = pos, axis, back
+        self.head, self.last = (TILES - 1, 0) if back else (0, TILES - 1)
         self.own, self.got, self.out, self.res, self.dec = own, got, out, res, dec
         self.ssem, self.rsem, self.slot = ssem, rsem, slot
 
@@ -151,7 +153,7 @@
 
     def copies(self, stage, part):
         out, piece = [], pl.ds(part * STATE, STATE)
-        for d in (4, 3, 5, 2, 6, 1, 7):
+        for d in ORDER:
             k, to = self.peer(d)
             sems = self.ssem.at[self.slot, stage, part, d], self.rsem.at[self.slot, stage, part, d]
             if stage == 0:
@@ -161,36 +163,51 @@
         return out
 
     def start(self, part):
-        for copy in self.copies(0, part):
-            copy.start()
+        @pl.when(self.me != self.last)
+        def _():
+            for copy in self.copies(0, part):
+                copy.start()
+
         self.got[self.me, pl.ds(part * STATE, STATE)] = self.own[self.lines(self.me, part)]
 
     def turn(self, part):
-        for copy in self.copies(0, part):
-            copy.wait_recv()
+        for d, copy in zip(ORDER, self.copies(0, part)):
+            pl.when(lax.rem(self.me - d + TILES, TILES) != self.last)(copy.wait_recv)
         state, piece = jnp.zeros((STATE, E), F32), pl.ds(part * STATE, STATE)
         for j in range(TILES - 1, -1, -1) if self.back else range(TILES):
             self.out[j, piece] = state
-            state = self.dec[pl.ds(j * SHARE + part * STATE, STATE)] * state + self.got[j, piece]
-        for copy in self.copies(1, part):
-            copy.start()
-        self.res[self.lines(self.me, part)] = self.out[self.me, piece]
+            if j != self.last:
+                state = self.dec[pl.ds(j * SHARE + part * STATE, STATE)] * state + self.got[j, piece]
+        for d, copy in zip(ORDER, self.copies(1, part)):
+            pl.when(self.peer(d)[0] != self.head)(copy.start)
 
     def finish(self):
+        @pl.when(self.me == self.head)
+        def _():
+            self.res[...] = jnp.zeros((T, E), F32)
+
+        @pl.when(self.me != self.head)
+        def _():
+            for part in range(PARTS):
+                self.res[self.lines(self.me, part)] = self.out[self.me, pl.ds(part * STATE, STATE)]
+                for copy in self.copies(1, part):
+                    copy.wait_recv()
+
+    def drain(self):
         for part in range(PARTS):
-            for copy in self.copies(1, part):
-                copy.wait_recv()
-
-    def drain(self):
-        for stage in (0, 1):
-            for part in range(PARTS):
-                for copy in self.copies(stage, part):
+            @pl.when(self.me != self.last)
+            def _():
+                for copy in self.copies(0, part):
                     copy.wait_send()
 
+            for d, copy in zip(ORDER, self.copies(1, part)):
+                pl.when(self.peer(d)[0] != self.head)(copy.wait_send)
+
 
 class Total:
-    def __init__(self, pos, buf, out, cbuf, xbuf, ybuf, zbuf, ssem, rsem):
+    def __init__(self, pos, buf, out, cbuf, xbuf, ybuf, zbuf, ssem, rsem, cuts):
         n = buf.shape[0]
+        self.cuts = cuts
         self.pos, self.buf, self.out = pos, buf, out
         self.cbuf, self.xbuf, self.ybuf, self.zbuf = cbuf, xbuf, ybuf, zbuf
         self.ssem, self.rsem = ssem, rsem
@@ -213,11 +230,17 @@
 
     def copies(self, stage):
         pos = self.pos
-        if stage in (0, 6):
-            src = self.buf.at[self.rows((1 - pos["co"]) * self.nh, self.nh)]
+        if stage == 0:
+            out, offset = [], 0
+            for k, size in enumerate(self.cuts):
+                src = self.buf.at[self.rows((1 - pos["co"]) * self.nh + offset, size)]
+                sems = self.ssem.at[0, k], self.rsem.at[0, k]
+                out.append(remote(src, self.cbuf.at[pl.ds(offset, size)], *sems, self.other))
+                offset += size
+            return out
+        if stage == 6:
             own = self.out.at[self.rows(self.base, self.nh)]
-            src, dst = (src, self.cbuf) if stage == 0 else (own, own)
-            return [remote(src, dst, self.ssem.at[stage, 0], self.rsem.at[stage, 0], self.other)]
+            return [remote(own, own, self.ssem.at[6, 0], self.rsem.at[6, 0], self.other)]
         out = []
         for p, (order, g0, g1, size, offset, start, first, second) in enumerate(self.parts):
             n0, n1 = size // 4, size // 16
@@ -294,7 +317,7 @@
     ("mr", vm(2, HEADS, T, T, dtype=BF16)), ("mc", vm(2, HEADS, T, T, dtype=BF16)), ("ls", vm(HEADS, T, T)),
     ("yr", vm(*BIG)), ("yc", vm(*BIG)), ("car", vm(*BIG)), ("cac", vm(*BIG)), ("dn", vm(*BIG)),
     ("dy", vm(*BIG)), ("dyb", vm(2, *BIG, dtype=BF16)), ("dzb", vm(*BIG, dtype=BF16)), ("nb", vm(*BIG, dtype=BF16)),
-    ("qr", vm(*BIG)), ("qc", vm(*BIG)), ("dxb", vm(*BIG, dtype=BF16)), ("dux", vm(*BIG)),
+    ("qr", vm(*BIG)), ("qc", vm(*BIG)), ("dxb", vm(*BIG, dtype=BF16)), ("act", vm(*BIG)), ("hd", vm(T, 128)), ("dux", vm(*BIG)),
     ("dbe", vm(T, T)), ("dce", vm(T, T)),
     ("own", pltpu.VMEM((4, T, E), F32)), ("got", pltpu.VMEM((4, TILES, SHARE, E), F32)),
     ("out", pltpu.VMEM((4, TILES, SHARE, E), F32)), ("res", pltpu.VMEM((4, T, E), F32)),
@@ -326,7 +349,7 @@
 def body(factor, tok_h, cot_h, wi_h, ws_h, bias_h, rate_h, skip_h, gain_h, wo_h, lo, gt, eres, lres,
          x, z, ub, stepe, bt, ct, s, ds, wsel, wpad, vecs, step, sig, cumr, cumc, cumrt, cumct,
          er, ec, wr, wc, dr, dc, dxr, dxc, finr, finc, allr, allc, wur, wuc, edr, edc, mr, mc, ls,
-         yr, yc, car, cac, dn, dy, dyb, dzb, nb, qr, qc, dxb, dux, dbe, dce,
+         yr, yc, car, cac, dn, dy, dyb, dzb, nb, qr, qc, dxb, act, hd, dux, dbe, dce,
          own, got, out, res, ebuf, ecb, exb, eyb, ezb, lbuf, lcb, lxb, lyb, lzb,
          fsem, cs, cr, es, erv, lsm, lrv, tok, cot, wi, ws, bias, rate, skip, gain, wo, isem):
     pos = place()
@@ -345,10 +368,10 @@
     near += [at(pos, xl=1 - pos["xl"]), at(pos, xl=1 - pos["xl"], xh=1 - pos["xh"])]
     for to in near:
         pl.semaphore_signal(barrier, inc=1, device_id=to, device_id_type=MESH)
-    early = Total(pos, ebuf, eres, ecb, exb, eyb, ezb, es, erv)
-    late = Total(pos, lbuf, lres, lcb, lxb, lyb, lzb, lsm, lrv)
-
-    for copy in fetch[:6]:
+    early = Total(pos, ebuf, eres, ecb, exb, eyb, ezb, es, erv, (EARLY // 2,))
+    late = Total(pos, lbuf, lres, lcb, lxb, lyb, lzb, lsm, lrv, (512, 128))
+
+    for copy in fetch[:5]:
         copy.wait()
     r, c = grid2(2 * STATE + HEADS, 640)
     sel = ((c < 256) & (r == lo4(c))) | ((c >= 256) & (c < 512) & (r == 16 + lo4(c))) | ((c >= 512) & (r == c - 480))
@@ -376,6 +399,7 @@
     stepe[...] = spread(stp, hx, 3)
     wr[...] = spread(jnp.exp(aft_r), hx)
     wc[...] = spread(jnp.exp(aft_c), hx)
+    fetch[5].wait()
     x[...] = mm(tok[...], wi[:, 0:E])
     keep(bt, (), mm(tok[...], wsel[:, 0:256]))
 
@@ -467,6 +491,15 @@
         fc.turn(part)
     lax.fori_loop(0, HEADS // 2, within, 0)
     dn[...] = mm(cot[...], wo[...], 1, 1)
+
+    def gate(sl, i, carry):
+        z_ = z[sl]
+        sg = 1.0 / (1.0 + jnp.exp(-z_))
+        act[sl] = z_ * sg
+        z[sl] = sg * (1.0 + z_ * (1.0 - sg))
+        return carry
+
+    loop(T, gate)
     fr.finish()
     car[...] = mm3(only(line_r, ct), split(res[0], 2))
     fc.finish()
@@ -477,21 +510,19 @@
 
     def middle(sl, i, carry):
         sum_gain, sum_skip = carry
-        x_, z_ = x[sl], z[sl]
+        x_, act_ = x[sl], act[sl]
         c_r, c_c = er[sl] * car[sl], ec[sl] * cac[sl]
         w_r, w_c = yr[sl], yc[sl]
         y = (w_r + w_c) + (c_r + c_c) + skipe * x_
-        sg = 1.0 / (1.0 + jnp.exp(-z_))
-        act = z_ * sg
-        gated = y * act
+        gated = y * act_
         inv = lax.rsqrt(jnp.mean(gated * gated, axis=-1, keepdims=True) + 1e-05)
         unit = gated * inv
         nb[sl] = (unit * gain_).astype(BF16)
         d_n = dn[sl]
         g1 = d_n * gain_
         dg = inv * (g1 - unit * jnp.mean(g1 * unit, axis=-1, keepdims=True))
-        d_y = dg * act
-        dzb[sl] = (dg * y * (sg * (1.0 + z_ * (1.0 - sg)))).astype(BF16)
+        d_y = dg * act_
+        dzb[sl] = (dg * y * z[sl]).astype(BF16)
         dy[sl] = d_y
         keep(dyb, (sl,), d_y)
         keep(edr, (sl,), er[sl] * d_y)
@@ -552,41 +583,58 @@
     )
     dbe[...] = jnp.where(head, mm3(d_s, both(ct), 0, 0), 0.0)
     lo[...] = mm(nb[...], wo[...]).astype(BF16)
+
+    def ahead(sl, i, carry):
+        x_, se = x[sl], stepe[sl]
+        u_ = se * x_
+        w_r, w_c = yr[sl], yc[sl]
+        w_ = w_r + w_c
+        qr[sl] = qr[sl] - u_ * w_r
+        qc[sl] = qc[sl] - u_ * w_c
+        dux[sl] = w_ * x_
+        dy[sl] = se * w_ + skipe * dy[sl]
+        res[0, sl] = own[0, sl] + dr[sl] * res[0, sl]
+        res[1, sl] = own[1, sl] + dc[sl] * res[1, sl]
+        return carry
+
+    loop(T, ahead)
+    cumr[...] = head_sum(qr[...])
+    cumc[...] = head_sum(qc[...])
+    hd[...] = head_sum(dux[...])
+    early.step(0)
     gr_.finish()
     g_r = split(res[2], 2)
     car[...] = mm3(only(line_r, bt), g_r)
     dbe[...] = dbe[...] + jnp.where(line_r, mm3(both(wur), g_r, 1, 1), 0.0)
     gc_.finish()
-    early.step(0)
     g_c = split(res[3], 2)
     cac[...] = mm3(only(line_c, bt), g_c)
     dbe[...] = dbe[...] + jnp.where(line_c, mm3(both(wuc), g_c, 1, 1), 0.0)
 
     def last(sl, i, carry):
-        x_, se = x[sl], stepe[sl]
-        u_ = se * x_
+        x_ = x[sl]
         v_r, v_c = wr[sl] * car[sl], wc[sl] * cac[sl]
-        w_r, w_c = yr[sl], yc[sl]
-        qr[sl] = qr[sl] - u_ * (v_r + w_r)
-        qc[sl] = qc[sl] - u_ * (v_c + w_c)
-        d_u = (w_r + w_c) + (v_r + v_c)
-        dux[sl] = d_u * x_
-        dxb[sl] = (se * d_u + skipe * dy[sl]).astype(BF16)
-        res[0, sl] = res[2, sl] * (own[0, sl] + dr[sl] * res[0, sl])
-        res[1, sl] = res[3, sl] * (own[1, sl] + dc[sl] * res[1, sl])
+        qr[sl] = x_ * v_r
+        qc[sl] = x_ * v_c
+        dxb[sl] = (dy[sl] + stepe[sl] * (v_r + v_c)).astype(BF16)
+        res[0, sl] = res[2, sl] * res[0, sl]
+        res[1, sl] = res[3, sl] * res[1, sl]
         return carry
 
     loop(T, last)
     lg = mm(tok[...], dxb[...], 0, 0) * factor
     for j in range(4):
         lbuf[LROW[j] : LROW[j] + 256] = lg[:, j * 128 : (j + 1) * 128]
+    late_core = late.copies(0)
+    late_core[0].start()
+    h_r, h_c = head_sum(qr[...]), head_sum(qc[...])
     d_a = (
-        pick(ind(same_r & (u >= t)), head_sum(qr[...]))
-        + pick(ind(same_c & (u >= t)), head_sum(qc[...]))
+        pick(ind(same_r & (u >= t)), cumr[...] - step[...] * h_r)
+        + pick(ind(same_c & (u >= t)), cumc[...] - step[...] * h_c)
         + pick(ind(line_r), head_sum(res[0]))
         + pick(ind(line_c), head_sum(res[1]))
     )
-    d_step = head_sum(dux[...]) - vecs[1:2, :] * d_a
+    d_step = hd[...] + (h_r + h_c) - vecs[1:2, :] * d_a
     d_raw = d_step * sig[...]
     r, c = grid2(T, 128)
     d_ssm = (
@@ -605,7 +653,7 @@
     lbuf[VROW + 4 : VROW + 5] = total_of(d_raw) * factor
     lbuf[VROW + 5 : VROW + 6] = -total_of(step[...] * d_a) * factor
     lbuf[VROW + 6 : VROW + 7] = total_of(head_sum(sum_skip)) * factor
-    late.start(0)
+    late_core[1].start()
     early.step(1)
     back = mm(dxb[...], wi[:, 0:E], 1, 1)
     late.step(0)

time: 76.9 us -> 74.6 us (0.970)
  Pallas kernels: 76.1 us -> 73.8 us
    pallas_call x1, Pallas kernels: 74.7 us -> 72.4 us  [local(): pl.pallas_call(functools.partial(kernel, factor), out_shape=(shape((T, D)...]
where the time goes in v5:
time: 74.6 us; the launch traced here: 74.5 us
  Pallas kernels  73.8 us (99%)
    pallas_call x1, Pallas kernels, local(): pl.pallas_call(functools.partial(kernel, factor), out_shape=(shape((T, D)...  72.4 us

profile of v5, /device:TPU:1, one launch (start us, length us, event | category | flops | bytes accessed | tf_op | source)
XLA Modules:
  0.0 74.5 jit_solution(2493402960917106393)
XLA Ops:
  0.6 72.4 %shard_map.160 = (bf16[256,256]{1,0:T(8,128)(2,1)S(1)}, bf16[256,256]{1,0:T(8,128)(2,1)S(1)}, f32[2048,128]{1,0:T(8,128)S(1)}, f32[1280,128]{1,0:T(8,128)S(1)}) custom-call(bf16[256,256]{1,0:T(8,128)(2,1)} %bitcast.14, bf16[256,256]{1,0:T(8,128)(2,1)} %bitcast.15, bf16[256,1024]{1,0:T(8,128)(2,1)} %refs_2_.1, bf16[40,256]{1,0:T(8,128)(2,1)} %bitcast.16, ...), custom_call_target="tpu_custom_call" | custom-call | tf_op jit(solution)/shard_map/pallas_call | solution.py:700
  73.0 1.5 %shard_map.161 = (bf16[256,256]{1,0:T(8,128)(2,1)}, bf16[256,256]{1,0:T(8,128)(2,1)}, f32[256,1024]{1,0:T(8,128)}, f32[40,256]{1,0:T(8,128)}, f32[512,256]{1,0:T...) custom-call(f32[2048,128]{1,0:T(8,128)S(1)} %get-tuple-element.22.eres, ...), custom_call_target="tpu_custom_call" | custom-call | tf_op jit(solution)/shard_map/pallas_call | solution.py:725

commit v6 on v5

--- a/solution.py
+++ b/solution.py
@@ -336,7 +336,7 @@
     ("skip", vm(1, HEADS)), ("gain", vm(1, E)), ("wo", vm(E, D, dtype=BF16)),
     ("isem", pltpu.SemaphoreType.DMA((9,))),
 ]
-RB = 32
+RB = 128
 
 
 def loop(rows, fn, init=0):

time: 74.6 us -> 73.6 us (0.987)
  Pallas kernels: 73.8 us -> 72.8 us
    pallas_call x1, Pallas kernels: 72.4 us -> 71.4 us  [local(): pl.pallas_call(functools.partial(kernel, factor), out_shape=(shape((T, D)...]
where the time goes in v6:
time: 73.6 us; the launch traced here: 73.5 us
  Pallas kernels  72.8 us (99%)
    pallas_call x1, Pallas kernels, local(): pl.pallas_call(functools.partial(kernel, factor), out_shape=(shape((T, D)...  71.4 us

profile of v6, /device:TPU:1, one launch (start us, length us, event | category | flops | bytes accessed | tf_op | source)
XLA Modules:
  0.0 73.5 jit_solution(4412475757779558297)
XLA Ops:
  0.6 71.4 %shard_map.160 = (bf16[256,256]{1,0:T(8,128)(2,1)S(1)}, bf16[256,256]{1,0:T(8,128)(2,1)S(1)}, f32[2048,128]{1,0:T(8,128)S(1)}, f32[1280,128]{1,0:T(8,128)S(1)}) custom-call(bf16[256,256]{1,0:T(8,128)(2,1)} %bitcast.14, bf16[256,256]{1,0:T(8,128)(2,1)} %bitcast.15, bf16[256,1024]{1,0:T(8,128)(2,1)} %refs_2_.1, bf16[40,256]{1,0:T(8,128)(2,1)} %bitcast.16, ...), custom_call_target="tpu_custom_call" | custom-call | tf_op jit(solution)/shard_map/pallas_call | solution.py:700
  72.0 1.5 %shard_map.161 = (bf16[256,256]{1,0:T(8,128)(2,1)}, bf16[256,256]{1,0:T(8,128)(2,1)}, f32[256,1024]{1,0:T(8,128)}, f32[40,256]{1,0:T(8,128)}, f32[512,256]{1,0:T...) custom-call(f32[2048,128]{1,0:T(8,128)S(1)} %get-tuple-element.22.eres, ...), custom_call_target="tpu_custom_call" | custom-call | tf_op jit(solution)/shard_map/pallas_call | solution.py:725

commit v7 on v6

--- a/solution.py
+++ b/solution.py
@@ -336,7 +336,7 @@
     ("skip", vm(1, HEADS)), ("gain", vm(1, E)), ("wo", vm(E, D, dtype=BF16)),
     ("isem", pltpu.SemaphoreType.DMA((9,))),
 ]
-RB = 128
+RB = 256
 
 
 def loop(rows, fn, init=0):

time: 73.6 us -> 73.4 us (level)
  no operation moved by 1% of the time
where the time goes in v7:
time: 73.4 us; the launch traced here: 73.3 us
  Pallas kernels  72.6 us (99%)
    pallas_call x1, Pallas kernels, local(): pl.pallas_call(functools.partial(kernel, factor), out_shape=(shape((T, D)...  71.2 us

profile of v7, /device:TPU:1, one launch (start us, length us, event | category | flops | bytes accessed | tf_op | source)
XLA Modules:
  0.0 73.3 jit_solution(15544912845899139834)
XLA Ops:
  0.6 71.2 %shard_map.160 = (bf16[256,256]{1,0:T(8,128)(2,1)S(1)}, bf16[256,256]{1,0:T(8,128)(2,1)S(1)}, f32[2048,128]{1,0:T(8,128)S(1)}, f32[1280,128]{1,0:T(8,128)S(1)}) custom-call(bf16[256,256]{1,0:T(8,128)(2,1)} %bitcast.14, bf16[256,256]{1,0:T(8,128)(2,1)} %bitcast.15, bf16[256,1024]{1,0:T(8,128)(2,1)} %refs_2_.1, bf16[40,256]{1,0:T(8,128)(2,1)} %bitcast.16, ...), custom_call_target="tpu_custom_call" | custom-call | tf_op jit(solution)/shard_map/pallas_call | solution.py:700
  71.8 1.5 %shard_map.161 = (bf16[256,256]{1,0:T(8,128)(2,1)}, bf16[256,256]{1,0:T(8,128)(2,1)}, f32[256,1024]{1,0:T(8,128)}, f32[40,256]{1,0:T(8,128)}, f32[512,256]{1,0:T...) custom-call(f32[2048,128]{1,0:T(8,128)S(1)} %get-tuple-element.22.eres, ...), custom_call_target="tpu_custom_call" | custom-call | tf_op jit(solution)/shard_map/pallas_call | solution.py:725
